TPU v7x, 32 devices: a whole 2x2x4 slice. The times are simulated.
32 devices in a mesh: tile: 16 (over z, y, core), seg: 2 (over x).
Axes of the slice: x: 2, y: 2, z: 4, core: 2. Of those that a mesh axis runs over, the one named last changes fastest.
Arguments:
- right_sides: float32 [65536, 512], P(('tile', 'seg')), may hold values from -6 to 6
- leaf_proj: float32 [16, 32, 64, 128], P('tile', 'seg'), may hold values from -0.5 to 0.5
- col_levels: float32 [16, 4, 16, 128, 128], P('tile', None, 'seg'), may hold values from -0.5 to 0.5
- middle_factor: float32 [16, 32, 64, 64], P('tile', 'seg'), may hold values from -0.75 to 0.75
- row_levels: float32 [16, 4, 16, 128, 128], P('tile', None, 'seg'), may hold values from -0.5 to 0.5
- leaf_expand: float32 [16, 32, 128, 64], P('tile', 'seg'), may hold values from -0.1875 to 0.1875
Outputs:
- product: float32 [4096, 512], P(('seg', 'tile'))
All inputs are finite; a program needn't handle non-finite values.
Results may differ from a plain program's by a relative error of at most 0.0001.
Values sent between devices are 32-bit elements; how exact they have to be, the bound alone decides.
No kernel may reach another device: no remote copies, remote signals or barrier semaphores. Data moves between devices by JAX's collectives and lax.ppermute only.
A program may use at most 64 MiB of HBM per device.

v0:
```python
import functools

import jax
import jax.numpy as jnp
from jax import lax
from jax.experimental import pallas as pl
from jax.experimental.pallas import tpu as pltpu
from jax.sharding import PartitionSpec as P

F32 = jnp.float32
BF16 = jnp.bfloat16
CHUNK = 128


def split(x):
    hi = x.astype(BF16)
    return hi, (x - hi.astype(F32)).astype(BF16)


def dot(a, b, dims=((1,), (0,))):
    return lax.dot_general(a, b, (dims, ((), ())), preferred_element_type=F32)


def wide_of(w):
    return jnp.concatenate(split(w), axis=1)


def product3(wide, v_hi, v_lo):
    depth, width = v_hi.shape
    if width > CHUNK:
        return dot(wide, jnp.concatenate([v_hi, v_hi], axis=0)) + dot(wide[:, :depth], v_lo)
    left = jnp.concatenate([v_hi, v_hi], axis=0)
    right = jnp.concatenate([v_lo, jnp.zeros_like(v_lo)], axis=0)
    both = dot(wide, jnp.concatenate([left, right], axis=1))
    return both[:, :width] + both[:, width:]


def pair_of(hi, lo, first, second, rank, cols=slice(None)):
    return [jnp.concatenate([x[pl.ds(first, rank), cols], x[pl.ds(second, rank), cols]], axis=0) for x in (hi, lo)]


def level_step(level, wide_at, hi, lo, rank, cuts):
    d = 2**level
    for j in range(hi.shape[0] // (2 * rank)):
        first = ((j // d) * 2 * d + j % d) * rank
        second = first + d * rank
        wide = wide_at(j)
        for cols in cuts:
            out_hi, out_lo = split(product3(wide, *pair_of(hi, lo, first, second, rank, cols)))
            for place, half in ((first, 0), (second, 1)):
                hi[pl.ds(place, rank), cols] = out_hi[half * rank:(half + 1) * rank]
                lo[pl.ds(place, rank), cols] = out_lo[half * rank:(half + 1) * rank]


def cuts_of(width):
    odd = width % (2 * CHUNK)
    return ([slice(0, odd)] if odd else []) + [slice(k, k + 2 * CHUNK) for k in range(odd, width, 2 * CHUNK)]


def project(n, wide, x, hi, lo, cuts):
    rank, leaf = wide.shape[0], wide.shape[1] // 2
    for cols in cuts:
        c_hi, c_lo = split(product3(wide, *split(x[n * leaf:(n + 1) * leaf, cols])))
        hi[n * rank:(n + 1) * rank, cols] = c_hi
        lo[n * rank:(n + 1) * rank, cols] = c_lo


def middle(n_seg, mid, outs, hi, lo, cuts):
    box, rank = mid.shape[:2]
    share = box // n_seg
    seg = lax.axis_index("seg")
    for delta in reversed(range(n_seg)):
        base = (seg ^ delta) * share
        for p in range(share):
            wide = wide_of(mid[base + p])
            at = pl.multiple_of((base + p) * rank, rank)
            for cols in cuts:
                out = product3(wide, hi[pl.ds(at, rank), cols], lo[pl.ds(at, rank), cols])
                for k in range(out.shape[1] // CHUNK):
                    target = outs[(cols.start // CHUNK + k) * n_seg + delta]
                    target[p * rank:(p + 1) * rank, :] = out[:, k * CHUNK:(k + 1) * CHUNK]


def column_kernel(n_seg, pieces, start, x_hbm, proj_hbm, col_hbm, mid_hbm, *refs):
    outs, (x_ref, proj_ref, col_ref, mid_ref, hi, lo, sems) = refs[:-7], refs[-7:]
    box, rank, leaf = proj_ref.shape
    levels, pairs = col_ref.shape[:2]
    width = x_ref.shape[1]
    per = box // pieces
    copies = []

    def fetch(src, dst):
        copies.append(pltpu.make_async_copy(src, dst, sems.at[len(copies)]))
        copies[-1].start()
        return copies[-1]

    first = []
    for k in range(pieces):
        rows = pl.ds(k * per * leaf, per * leaf)
        leaves = pl.ds(k * per, per)
        first.append((
            fetch(proj_hbm.at[leaves], proj_ref.at[leaves]),
            fetch(x_hbm.at[rows, pl.ds(start, width)], x_ref.at[rows, :]),
        ))
    halves = [pl.ds(k * (pairs // 2), pairs // 2) for k in range(2)]
    cols = [[fetch(col_hbm.at[k, h], col_ref.at[k, h]) for h in halves] for k in range(levels)]
    mid = fetch(mid_hbm, mid_ref)

    cuts = cuts_of(width)
    for k in range(pieces):
        for copy in first[k]:
            copy.wait()
        for n in range(k * per, (k + 1) * per):
            project(n, wide_of(proj_ref[n]), x_ref, hi, lo, cuts)
    for level in range(levels):
        for copy in cols[level]:
            copy.wait()
        level_step(level, lambda j: wide_of(col_ref[level, j]), hi, lo, rank, cuts)
    mid.wait()
    middle(n_seg, mid_ref, outs, hi, lo, cuts)


def slots_of(n_tile, box, leaf):
    bits = n_tile.bit_length() - 1
    out_rows = box * leaf // n_tile
    relative = [int(format(slot, f"0{bits}b")[::-1], 2) for slot in range(n_tile)]
    return relative, out_rows, min(out_rows, leaf), max(1, out_rows // leaf)


def weights_kernel(row_ref, wide_ref):
    for level in range(row_ref.shape[0]):
        for j in range(row_ref.shape[1]):
            wide_ref[level, j] = wide_of(row_ref[level, j])


def expand_weights_kernel(n_tile, exp_ref, other_ref, last_ref):
    box, _, leaf = exp_ref.shape
    tile = lax.axis_index("tile")
    relative, out_rows, unit, pieces = slots_of(n_tile, box, leaf)
    for slot in range(n_tile // 2):
        block = tile ^ relative[slot]
        for piece in range(pieces):
            n = (block * out_rows + piece * unit) // leaf
            both = jnp.concatenate([exp_ref[n], other_ref[n]], axis=0).T
            rows = both[:unit]
            for k in range(1, leaf // unit):
                rows = jnp.where(block % (leaf // unit) == k, both[k * unit:(k + 1) * unit], rows)
            last_ref[slot * pieces + piece] = wide_of(rows)


def row_kernel(n_seg, n_tile, leaf, *refs):
    ins, (row_ref, *outs, hi, lo, full) = refs[:n_seg], refs[n_seg:]
    levels, pairs = row_ref.shape[:2]
    box = 2 * pairs
    rank = hi.shape[0] // box
    share = box // n_seg
    seg = lax.axis_index("seg")
    tile = lax.axis_index("tile")
    for delta in range(n_seg):
        base = (seg ^ delta) * share
        at = pl.multiple_of(base * rank, share * rank)
        v_hi, v_lo = split(ins[delta][...])
        hi[pl.ds(at, share * rank), :] = v_hi
        lo[pl.ds(at, share * rank), :] = v_lo
    for level in range(levels - 1):
        level_step(level, lambda j: row_ref[level, j], hi, lo, rank, [slice(None)])
    for j in range(pairs):
        second = (j + pairs) * rank
        out = product3(row_ref[levels - 1, j], *pair_of(hi, lo, j * rank, second, rank))
        full[j * rank:(j + 1) * rank, :] = out[:rank]
        full[second:second + rank, :] = out[rank:]
    relative, out_rows, unit, pieces = slots_of(n_tile, box, leaf)
    group = n_tile // 4
    for slot in range(n_tile):
        block = tile ^ relative[slot]
        for piece in range(pieces):
            n = (block * out_rows + piece * unit) // leaf
            at = (slot % group * pieces + piece) * rank
            outs[slot // group][at:at + rank, :] = full[pl.ds(pl.multiple_of(n * rank, rank), rank), :]


def expand_kernel(part, own_ref, other_ref, last_ref, out_ref):
    rank = last_ref.shape[2] // 4
    unit = last_ref.shape[1]
    for k in range(own_ref.shape[0] // rank):
        rows = slice(k * rank, (k + 1) * rank)
        v = jnp.concatenate([own_ref[rows, :], other_ref[rows, :]], axis=0)
        wide = last_ref[part * own_ref.shape[0] // rank + k]
        out_ref[k * unit:(k + 1) * unit, :] = product3(wide, *split(v))


def tie(x, *others):
    return lax.optimization_barrier((x, *others))[0]


def shards(n_tile, n_seg, right_sides, leaf_proj, col_levels, middle_factor, row_levels, leaf_expand):
    proj, col, mid, row = leaf_proj[0], col_levels[0], middle_factor[0], row_levels[0]
    expand = jnp.swapaxes(leaf_expand[0], 1, 2)
    box, rank, leaf = proj.shape
    levels, pairs = col.shape[:2]
    chunks = right_sides.shape[1] // CHUNK
    _, out_rows, unit, pieces = slots_of(n_tile, box, leaf)
    bits = n_tile.bit_length() - 1
    part = jax.ShapeDtypeStruct((box * rank // n_seg, CHUNK), F32)
    quarter = jax.ShapeDtypeStruct((n_tile // 4 * pieces * rank, CHUNK), F32)
    summed = jax.ShapeDtypeStruct((box * leaf // 4, CHUNK), F32)
    params = pltpu.CompilerParams(vmem_limit_bytes=16 * 2**20)
    cost = pl.CostEstimate(flops=1_000_000, bytes_accessed=100_000, transcendentals=0)
    in_hbm = pl.BlockSpec(memory_space=pltpu.HBM)
    in_vmem = pl.BlockSpec(memory_space=pltpu.VMEM)

    def column_side(start, count, mid, limit):
        pieces = 4
        width = count * CHUNK
        outs = pl.pallas_call(
            functools.partial(column_kernel, n_seg, pieces, start * CHUNK),
            in_specs=[in_hbm] * 4,
            out_specs=[in_vmem] * (n_seg * count),
            out_shape=[part] * (n_seg * count),
            scratch_shapes=[
                pltpu.VMEM((box * leaf, width), F32),
                pltpu.VMEM(proj.shape, F32),
                pltpu.VMEM(col.shape, F32),
                pltpu.VMEM(mid.shape, F32),
                pltpu.VMEM((box * rank, width), BF16),
                pltpu.VMEM((box * rank, width), BF16),
                pltpu.SemaphoreType.DMA((2 * pieces + 2 * levels + 1,)),
            ],
            compiler_params=pltpu.CompilerParams(vmem_limit_bytes=limit * 2**20),
            cost_estimate=cost,
            name="column_side",
        )(right_sides, proj, col, mid)
        return [outs[k * n_seg:(k + 1) * n_seg] for k in range(count)]

    def row_weights():
        return pl.pallas_call(
            weights_kernel,
            in_specs=[in_vmem],
            out_specs=in_vmem,
            out_shape=jax.ShapeDtypeStruct((levels, pairs, 2 * rank, 4 * rank), BF16),
            compiler_params=params,
            cost_estimate=cost,
            name="row_weights",
        )(row)

    def expand_weights(other):
        return pl.pallas_call(
            functools.partial(expand_weights_kernel, n_tile),
            in_specs=[in_vmem] * 2,
            out_specs=in_vmem,
            out_shape=jax.ShapeDtypeStruct((n_tile // 2 * pieces, unit, 4 * rank), BF16),
            compiler_params=params,
            cost_estimate=cost,
            name="expand_weights",
        )(expand, other)

    def row_side(parts, wide):
        return pl.pallas_call(
            functools.partial(row_kernel, n_seg, n_tile, leaf),
            in_specs=[in_vmem] * (n_seg + 1),
            out_specs=[in_vmem] * 4,
            out_shape=[quarter] * 4,
            scratch_shapes=[pltpu.VMEM((box * rank, CHUNK), t) for t in (BF16, BF16, F32)],
            compiler_params=params,
            cost_estimate=pl.CostEstimate(flops=20_000_000_000, bytes_accessed=100_000, transcendentals=0),
            name="row_side",
        )(*parts, wide)

    def expanded(part, own, other, last):
        return pl.pallas_call(
            functools.partial(expand_kernel, part),
            in_specs=[in_vmem] * 3,
            out_specs=in_vmem,
            out_shape=summed,
            compiler_params=params,
            cost_estimate=pl.CostEstimate(flops=(1 - part) * 2_000_000_000 + 1, bytes_accessed=100_000, transcendentals=0),
            name="expand",
        )(own, other, last)

    def swap(x, axis, size, mask):
        return lax.ppermute(x, axis, [(i, i ^ mask) for i in range(size)])

    def exchange(parts, *after):
        return [parts[0]] + [swap(tie(parts[k], *after) if after else parts[k], "seg", n_seg, k) for k in range(1, n_seg)]

    def total(terms, low, high):
        return functools.reduce(jnp.add, [x[low:high] for x in terms])

    def next_send(terms):
        left = terms[-1].shape[0]
        return total(terms, left // 2, left)

    parts = column_side(0, 1, mid, 53)
    received = {0: exchange(parts[0])}
    parts += column_side(1, chunks - 1, tie(mid, parts[0][-1]), 52)
    received[1] = exchange(parts[1])
    wide = row_weights()
    last_wide = expand_weights(swap(tie(expand, parts[-1][0]), "tile", n_tile, 1))

    terms, sends, lows = [], {}, []
    last = chunks - 1

    def forward(c, b, *after):
        terms[c][-1] = tie(terms[c][-1], *after)
        sends[c, b] = next_send(terms[c])
        terms[c].append(swap(sends[c, b], "tile", n_tile, 1 << b))
        return sends[c, b]

    def low_half(c, *after):
        own, other = lows[c]
        terms[c][0] = expanded(0, own, tie(other, *after), last_wide)
        return terms[c][0]

    for c in range(chunks):
        after = sends[c - 1, 1] if c else parts[-1][0]
        own_low, own_high, low, high = row_side([tie(x, after) for x in received[c]], wide)
        lows.append((own_low, swap(low, "tile", n_tile, 1)))
        done = []
        if c >= 1:
            done.append(low_half(c - 1, own_high))
        if c >= 2:
            done.append(forward(c - 2, 2, own_high))
        if c >= 3 and bits > 3:
            done.append(forward(c - 3, 3, own_high))
        got = swap(high, "tile", n_tile, 1)
        if done:
            got = tie(got, *done)
        sends[c, 1] = expanded(1, own_high, got, last_wide)
        terms.append([None, swap(sends[c, 1], "tile", n_tile, 2)])
        if c + 2 < chunks:
            received[c + 2] = exchange(parts[c + 2], sends[c, 1])
    low_half(last, sends[last, 1])
    done = [forward(last - 1, 2, sends[last, 1])]
    if bits > 3:
        done += [forward(k, 3, sends[last, 1]) for k in range(max(0, last - 2), last)]
    forward(last, 2, *done)
    for b in range(3, bits):
        for c in range(chunks):
            if (c, b) not in sends:
                forward(c, b, sends[last, 2])
    for c in range(last):
        terms[c][-1] = tie(terms[c][-1], sends[last, 2])
    return jnp.concatenate([total(t, 0, out_rows) for t in terms], axis=1)


def solution(mesh):
    in_specs = (
        P(("tile", "seg"), None),
        P("tile", "seg", None, None),
        P("tile", None, "seg", None, None),
        P("tile", "seg", None, None),
        P("tile", None, "seg", None, None),
        P("tile", "seg", None, None),
    )
    out_specs = P(("seg", "tile"), None)
    body = functools.partial(shards, mesh.shape["tile"], mesh.shape["seg"])
    return jax.shard_map(body, mesh=mesh, in_specs=in_specs, out_specs=out_specs, check_vma=False)
```

profile of v0, /device:TPU:0, one launch (start us, length us, event | category | flops | bytes accessed | tf_op | source)
XLA Modules:
  0.0 61.7 jit_solution(13462055304230887608)
XLA Ops:
  0.0 3.7 %column_side.2 = (f32[512,128]{1,0:T(8,128)S(1)}, f32[512,128]{1,0:T(8,128)S(1)}) custom-call(f32[2048,512]{1,0:T(8,128)} %x_hbm.3, f32[16,64,128]{2,1,0:T(8,128)} %bitcast.12, f32[4,8,128,128]{3,2,1,0:T(8,128)} %bitcast.10, f32[16,64,64]{2,1,0:T(8,128)} %bitcast.14), custom_call_target="tpu_custom_call" | custom-call | flops 1000000 | bytes 100000 | tf_op jit(solution)/shard_map/column_side/pallas_call | solution.py:215
  3.7 0.0 copy-start.1
  3.7 0.0 copy-start
  3.7 3.0 %collective-permute-start = (f32[512,128]{1,0:T(8,128)S(1)}, f32[512,128]{1,0:T(8,128)S(1)}, u32[]{:S(2)}, u32[]{:S(2)}) collective-permute-start(f32[512,128]{1,0:T(8,128)S(1)} %get-tuple-element.60), channel_id=1, source_target_pairs={{0,1},{1,0},{2,3},{3,2},{4,5},{5,4},{6,7},{7,6},{8,9},{9,8},{10,11... | collective-permute-start | bytes 786440 | tf_op jit(solution)/shard_map/ppermute | solution.py:281
  6.7 5.8 %column_side.3 = (f32[512,128]{1,0:T(8,128)S(1)}, f32[512,128]{1,0:T(8,128)S(1)}, f32[512,128]{1,0:T(8,128)S(1)}, f32[512,128]{1,0:T(8,128)S(1)}, f32[512,128]{1,0:T(8,128)S(1)}, /*index=5*/f32[512,128]{1,0:T(8,128)S(1)}) custom-call(f32[2048,512]{1,0:T(8,128)} %x_hbm.3, f32[16,64,128]{2,1,0:T(8,128)} %bitcast.13, f32[4,8,128,128]{3,2,1,0:T(8,128)} %bitcast.11, ...), custom_call_target="tpu_custom_call" | custom-call | flops 1000000 | bytes 100000 | tf_op jit(solution)/shard_map/column_side/pallas_call | solution.py:215
  12.5 0.2 collective-permute-start.4
  12.8 0.0 collective-permute-start.3
  12.8 0.3 row_weights.1.refs_2_
  13.0 0.0 collective-permute-done.refs_1_
  13.1 1.2 %row_side.4 = (f32[256,128]{1,0:T(8,128)S(1)}, f32[256,128]{1,0:T(8,128)S(1)}, f32[256,128]{1,0:T(8,128)S(1)}, f32[256,128]{1,0:T(8,128)S(1)}) custom-call(f32[512,128]{1,0:T(8,128)S(1)} %get-tuple-element.63.refs_0_, f32[512,128]{1,0:T(8,128)S(1)} %collective-permute-done.refs_1_, bf16[4,8,128,256]{3,2,1,0:T(8,128)(2,1)S(1)} %row_weights.1.refs_2_), custom_call_target="tpu_custom_call" | custom-call | flops 20000000000 | bytes 100000 | tf_op jit(solution)/shard_map/row_side/pallas_call | solution.py:258
  14.2 0.6 collective-permute-start.2
  14.8 0.1 collective-permute-start.1
  14.9 0.0 collective-permute-done.3.other_ref
  14.9 0.2 expand_weights.1.last_ref
  15.1 0.7 %collective-permute-done.2.other_ref = f32[256,128]{1,0:T(8,128)S(1)} collective-permute-done((f32[256,128]{1,0:T(8,128)S(1)}, f32[256,128]{1,0:T(8,128)S(1)}, u32[]{:S(2)}, u32[]{:S(2)}) %collective-permute-start.2) | collective-permute-done | bytes 131104 | tf_op jit(solution)/shard_map/ppermute | solution.py:281
  15.8 0.2 expand.8
  16.0 2.1 %collective-permute-start.5 = (f32[512,128]{1,0:T(8,128)S(1)}, f32[512,128]{1,0:T(8,128)S(1)}, u32[]{:S(2)}, u32[]{:S(2)}) collective-permute-start(f32[512,128]{1,0:T(8,128)S(1)} %expand.8), channel_id=1, source_target_pairs={{0,4},{2,6},{4,0},{6,2},{8,12},{10,14},{12,8},{14,10},{16,20},{18,... | collective-permute-start | bytes 786440 | tf_op jit(solution)/shard_map/ppermute | solution.py:281
  18.2 2.2 %collective-permute-done.4.refs_1_ = f32[512,128]{1,0:T(8,128)S(1)} collective-permute-done((f32[512,128]{1,0:T(8,128)S(1)}, f32[512,128]{1,0:T(8,128)S(1)}, u32[]{:S(2)}, u32[]{:S(2)}) %collective-permute-start.4) | collective-permute-done | bytes 262176 | tf_op jit(solution)/shard_map/ppermute | solution.py:281
  20.4 0.4 collective-permute-start.7
  20.8 1.2 %row_side.5 = (f32[256,128]{1,0:T(8,128)S(1)}, f32[256,128]{1,0:T(8,128)S(1)}, f32[256,128]{1,0:T(8,128)S(1)}, f32[256,128]{1,0:T(8,128)S(1)}) custom-call(f32[512,128]{1,0:T(8,128)S(1)} %get-tuple-element.71.refs_0_, f32[512,128]{1,0:T(8,128)S(1)} %collective-permute-done.4.refs_1_, bf16[4,8,128,256]{3,2,1,0:T(8,128)(2,1)S(1)} %row_weights.1.refs_2_), custom_call_target="tpu_custom_call" | custom-call | flops 20000000000 | bytes 100000 | tf_op jit(solution)/shard_map/row_side/pallas_call | solution.py:258
  22.0 0.0 collective-permute-done.1.other_ref
  22.0 0.1 collective-permute-start.6
  22.1 0.5 collective-permute-start.10
  22.6 0.2 expand.9
  22.8 0.6 collective-permute-done.6.other_ref
  23.4 0.2 expand.10
  23.7 1.8 %collective-permute-start.16 = (f32[512,128]{1,0:T(8,128)S(1)}, f32[512,128]{1,0:T(8,128)S(1)}, u32[]{:S(2)}, u32[]{:S(2)}) collective-permute-start(f32[512,128]{1,0:T(8,128)S(1)} %expand.10), channel_id=1, source_target_pairs={{0,4},{2,6},{4,0},{6,2},{8,12},{10,14},{12,8},{14,10},{16,20},{18,... | collective-permute-start | bytes 786440 | tf_op jit(solution)/shard_map/ppermute | solution.py:281
  25.5 1.3 %collective-permute-start.11 = (f32[512,128]{1,0:T(8,128)S(1)}, f32[512,128]{1,0:T(8,128)S(1)}, u32[]{:S(2)}, u32[]{:S(2)}) collective-permute-start(f32[512,128]{1,0:T(8,128)S(1)} %get-tuple-element.92), channel_id=1, source_target_pairs={{0,1},{1,0},{2,3},{3,2},{4,5},{5,4},{6,7},{7,6},{8,9},{9,8},{10,11... | collective-permute-start | bytes 786440 | tf_op jit(solution)/shard_map/ppermute | solution.py:281
  26.8 0.4 collective-permute-done.7.refs_1_
  27.2 1.2 %row_side.6 = (f32[256,128]{1,0:T(8,128)S(1)}, f32[256,128]{1,0:T(8,128)S(1)}, f32[256,128]{1,0:T(8,128)S(1)}, f32[256,128]{1,0:T(8,128)S(1)}) custom-call(f32[512,128]{1,0:T(8,128)S(1)} %get-tuple-element.79.refs_0_, f32[512,128]{1,0:T(8,128)S(1)} %collective-permute-done.7.refs_1_, bf16[4,8,128,256]{3,2,1,0:T(8,128)(2,1)S(1)} %row_weights.1.refs_2_), custom_call_target="tpu_custom_call" | custom-call | flops 20000000000 | bytes 100000 | tf_op jit(solution)/shard_map/row_side/pallas_call | solution.py:258
  28.4 0.1 collective-permute-start.9
  28.5 0.5 collective-permute-start.15
  29.0 1.6 %collective-permute-start.8 = (f32[256,128]{1,0:T(8,128)S(1)}, f32[256,128]{1,0:T(8,128)S(1)}, u32[]{:S(2)}, u32[]{:S(2)}) collective-permute-start(f32[256,128]{1,0:T(8,128)S(1)} %slice_add_fusion.3), channel_id=1, source_target_pairs={{0,8},{2,10},{4,12},{6,14},{8,0},{10,2},{12,4},{14,6},{16,24},{18,... | collective-permute-start | bytes 393224 | tf_op jit(solution)/shard_map/ppermute | solution.py:281
  30.7 0.2 expand.11
  30.9 0.0 collective-permute-done.9.other_ref
  30.9 0.2 expand.12
  31.2 1.8 %collective-permute-start.18 = (f32[512,128]{1,0:T(8,128)S(1)}, f32[512,128]{1,0:T(8,128)S(1)}, u32[]{:S(2)}, u32[]{:S(2)}) collective-permute-start(f32[512,128]{1,0:T(8,128)S(1)} %expand.12), channel_id=1, source_target_pairs={{0,4},{2,6},{4,0},{6,2},{8,12},{10,14},{12,8},{14,10},{16,20},{18,... | collective-permute-start | bytes 786440 | tf_op jit(solution)/shard_map/ppermute | solution.py:281
  33.0 0.6 %collective-permute-done.11.refs_1_ = f32[512,128]{1,0:T(8,128)S(1)} collective-permute-done((f32[512,128]{1,0:T(8,128)S(1)}, f32[512,128]{1,0:T(8,128)S(1)}, u32[]{:S(2)}, u32[]{:S(2)}) %collective-permute-start.11) | collective-permute-done | bytes 262176 | tf_op jit(solution)/shard_map/ppermute | solution.py:281
  33.6 1.2 %row_side.7 = (f32[256,128]{1,0:T(8,128)S(1)}, f32[256,128]{1,0:T(8,128)S(1)}, f32[256,128]{1,0:T(8,128)S(1)}, f32[256,128]{1,0:T(8,128)S(1)}) custom-call(f32[512,128]{1,0:T(8,128)S(1)} %get-tuple-element.90.refs_0_, f32[512,128]{1,0:T(8,128)S(1)} %collective-permute-done.11.refs_1_, bf16[4,8,128,256]{3,2,1,0:T(8,128)(2,1)S(1)} %row_weights.1.refs_2_), custom_call_target="tpu_custom_call" | custom-call | flops 20000000000 | bytes 100000 | tf_op jit(solution)/shard_map/row_side/pallas_call | solution.py:258
  34.8 0.0 collective-permute-done.16
  34.8 1.6 %collective-permute-start.19 = (f32[256,128]{1,0:T(8,128)S(1)}, f32[256,128]{1,0:T(8,128)S(1)}, u32[]{:S(2)}, u32[]{:S(2)}) collective-permute-start(f32[256,128]{1,0:T(8,128)S(1)} %slice_add_fusion.2), channel_id=1, source_target_pairs={{0,8},{2,10},{4,12},{6,14},{8,0},{10,2},{12,4},{14,6},{16,24},{18,... | collective-permute-start | bytes 393224 | tf_op jit(solution)/shard_map/ppermute | solution.py:281
  36.5 0.0 collective-permute-start.13
  36.5 0.5 collective-permute-start.14
  37.0 0.0 collective-permute-done.8
  37.0 2.7 %collective-permute-start.12 = (f32[128,128]{1,0:T(8,128)S(1)}, f32[128,128]{1,0:T(8,128)S(1)}, u32[]{:S(2)}, u32[]{:S(2)}) collective-permute-start(f32[128,128]{1,0:T(8,128)S(1)} %fusion.9), channel_id=1, source_target_pairs={{0,16},{2,18},{4,20},{6,22},{8,24},{10,26},{12,28},{14,30},{16,0},... | collective-permute-start | bytes 196616 | tf_op jit(solution)/shard_map/ppermute | solution.py:281
  39.6 0.2 expand.13
  39.9 0.0 collective-permute-done.14.other_ref
  39.9 0.2 expand.14
  40.1 0.8 %collective-permute-start.17 = (f32[512,128]{1,0:T(8,128)S(1)}, f32[512,128]{1,0:T(8,128)S(1)}, u32[]{:S(2)}, u32[]{:S(2)}) collective-permute-start(f32[512,128]{1,0:T(8,128)S(1)} %expand.14), channel_id=1, source_target_pairs={{0,4},{2,6},{4,0},{6,2},{8,12},{10,14},{12,8},{14,10},{16,20},{18,... | collective-permute-start | bytes 786440 | tf_op jit(solution)/shard_map/ppermute | solution.py:281
  41.0 0.0 collective-permute-done.19
  41.0 0.0 collective-permute-done.13.other_ref
  41.0 2.2 %collective-permute-start.21 = (f32[128,128]{1,0:T(8,128)S(1)}, f32[128,128]{1,0:T(8,128)S(1)}, u32[]{:S(2)}, u32[]{:S(2)}) collective-permute-start(f32[128,128]{1,0:T(8,128)S(1)} %fusion.8), channel_id=1, source_target_pairs={{0,16},{2,18},{4,20},{6,22},{8,24},{10,26},{12,28},{14,30},{16,0},... | collective-permute-start | bytes 196616 | tf_op jit(solution)/shard_map/ppermute | solution.py:281
  43.2 0.0 collective-permute-done.18
  43.2 1.8 %collective-permute-start.20 = (f32[256,128]{1,0:T(8,128)S(1)}, f32[256,128]{1,0:T(8,128)S(1)}, u32[]{:S(2)}, u32[]{:S(2)}) collective-permute-start(f32[256,128]{1,0:T(8,128)S(1)} %slice_add_fusion), channel_id=1, source_target_pairs={{0,8},{2,10},{4,12},{6,14},{8,0},{10,2},{12,4},{14,6},{16,24},{18,... | collective-permute-start | bytes 393224 | tf_op jit(solution)/shard_map/ppermute | solution.py:281
  45.0 0.2 expand.15
  45.3 3.1 %collective-permute-done.20 = f32[256,128]{1,0:T(8,128)S(1)} collective-permute-done((f32[256,128]{1,0:T(8,128)S(1)}, f32[256,128]{1,0:T(8,128)S(1)}, u32[]{:S(2)}, u32[]{:S(2)}) %collective-permute-start.20) | collective-permute-done | bytes 131104 | tf_op jit(solution)/shard_map/ppermute | solution.py:281
  48.4 1.0 %collective-permute-start.22 = (f32[128,128]{1,0:T(8,128)S(1)}, f32[128,128]{1,0:T(8,128)S(1)}, u32[]{:S(2)}, u32[]{:S(2)}) collective-permute-start(f32[128,128]{1,0:T(8,128)S(1)} %fusion.7), channel_id=1, source_target_pairs={{0,16},{2,18},{4,20},{6,22},{8,24},{10,26},{12,28},{14,30},{16,0},... | collective-permute-start | bytes 196616 | tf_op jit(solution)/shard_map/ppermute | solution.py:281
  49.4 0.0 collective-permute-done.17
  49.5 1.6 %collective-permute-start.23 = (f32[256,128]{1,0:T(8,128)S(1)}, f32[256,128]{1,0:T(8,128)S(1)}, u32[]{:S(2)}, u32[]{:S(2)}) collective-permute-start(f32[256,128]{1,0:T(8,128)S(1)} %slice_add_fusion.1), channel_id=1, source_target_pairs={{0,8},{2,10},{4,12},{6,14},{8,0},{10,2},{12,4},{14,6},{16,24},{18,... | collective-permute-start | bytes 393224 | tf_op jit(solution)/shard_map/ppermute | solution.py:281
  51.1 2.6 %collective-permute-done.22 = f32[128,128]{1,0:T(8,128)S(1)} collective-permute-done((f32[128,128]{1,0:T(8,128)S(1)}, f32[128,128]{1,0:T(8,128)S(1)}, u32[]{:S(2)}, u32[]{:S(2)}) %collective-permute-start.22) | collective-permute-done | bytes 65568 | tf_op jit(solution)/shard_map/ppermute | solution.py:281
  53.7 1.3 %collective-permute-done.23 = f32[256,128]{1,0:T(8,128)S(1)} collective-permute-done((f32[256,128]{1,0:T(8,128)S(1)}, f32[256,128]{1,0:T(8,128)S(1)}, u32[]{:S(2)}, u32[]{:S(2)}) %collective-permute-start.23) | collective-permute-done | bytes 131104 | tf_op jit(solution)/shard_map/ppermute | solution.py:281
  55.1 1.9 %collective-permute-start.24 = (f32[128,128]{1,0:T(8,128)S(1)}, f32[128,128]{1,0:T(8,128)S(1)}, u32[]{:S(2)}, u32[]{:S(2)}) collective-permute-start(f32[128,128]{1,0:T(8,128)S(1)} %fusion), channel_id=1, source_target_pairs={{0,16},{2,18},{4,20},{6,22},{8,24},{10,26},{12,28},{14,30},{16,0},... | collective-permute-start | bytes 196616 | tf_op jit(solution)/shard_map/ppermute | solution.py:281
  57.0 4.0 %collective-permute-done.24 = f32[128,128]{1,0:T(8,128)S(1)} collective-permute-done((f32[128,128]{1,0:T(8,128)S(1)}, f32[128,128]{1,0:T(8,128)S(1)}, u32[]{:S(2)}, u32[]{:S(2)}) %collective-permute-start.24) | collective-permute-done | bytes 65568 | tf_op jit(solution)/shard_map/ppermute | solution.py:281
  61.0 0.7 %pad_maximum_fusion = f32[128,512]{1,0:T(8,128)} fusion(f32[128,128]{1,0:T(8,128)S(1)} %fusion.2, f32[128,128]{1,0:T(8,128)S(1)} %fusion.4, f32[128,128]{1,0:T(8,128)S(1)} %fusion.6, f32[128,128]{1,0:T(8,128)S(1)} %fusion.11), kind=kLoop, calls=%fused_computation | loop fusion | flops 196608 | bytes 524288 | tf_op jit(solution)/shard_map/concatenate | solution.py:343
  (19 shorter events, 0.2 us)
Async XLA Ops:
  3.7 9.1 %copy-start.1 = (f32[1,16,128,64]{2,3,1,0:T(8,128)S(1)}, f32[1,16,128,64]{2,3,1,0:T(8,128)}, u32[]{:S(2)}) copy-start(f32[1,16,128,64]{2,3,1,0:T(8,128)} %param.11) | copy-start | bytes 1572868
  3.7 9.1 %copy-start = (f32[1,4,8,128,128]{4,3,2,1,0:T(8,128)S(1)}, f32[1,4,8,128,128]{4,3,2,1,0:T(8,128)}, u32[]{:S(2)}) copy-start(f32[1,4,8,128,128]{4,3,2,1,0:T(8,128)} %param.10) | copy-start | bytes 6291460
  3.7 9.3 %collective-permute-start = (f32[512,128]{1,0:T(8,128)S(1)}, f32[512,128]{1,0:T(8,128)S(1)}, u32[]{:S(2)}, u32[]{:S(2)}) collective-permute-start(f32[512,128]{1,0:T(8,128)S(1)} %get-tuple-element.60), channel_id=1, source_target_pairs={{0,1},{1,0},{2,3},{3,2},{4,5},{5,4},{6,7},{7,6},{8,9},{9,8},{10,11... | collective-permute-start | bytes 786440 | tf_op jit(solution)/shard_map/ppermute | solution.py:281
  12.5 7.8 %collective-permute-start.4 = (f32[512,128]{1,0:T(8,128)S(1)}, f32[512,128]{1,0:T(8,128)S(1)}, u32[]{:S(2)}, u32[]{:S(2)}) collective-permute-start(f32[512,128]{1,0:T(8,128)S(1)} %get-tuple-element.72), channel_id=1, source_target_pairs={{0,1},{1,0},{2,3},{3,2},{4,5},{5,4},{6,7},{7,6},{8,9},{9,8},{10,11... | collective-permute-start | bytes 786440 | tf_op jit(solution)/shard_map/ppermute | solution.py:281
  12.8 2.1 %collective-permute-start.3 = (f32[16,64,128]{2,1,0:T(8,128)S(1)}, f32[16,64,128]{2,1,0:T(8,128)S(1)}, u32[]{:S(2)}, u32[]{:S(2)}) collective-permute-start(f32[16,64,128]{2,1,0:T(8,128)S(1)} %bitcast.8), channel_id=1, source_target_pairs={{0,2},{2,0},{4,6},{6,4},{8,10},{10,8},{12,14},{14,12},{16,18},{18,... | collective-permute-start | bytes 1572872 | tf_op jit(solution)/shard_map/ppermute | solution.py:281
  14.2 1.6 %collective-permute-start.2 = (f32[256,128]{1,0:T(8,128)S(1)}, f32[256,128]{1,0:T(8,128)S(1)}, u32[]{:S(2)}, u32[]{:S(2)}) collective-permute-start(f32[256,128]{1,0:T(8,128)S(1)} %get-tuple-element.69), channel_id=1, source_target_pairs={{0,2},{2,0},{4,6},{6,4},{8,10},{10,8},{12,14},{14,12},{16,18},{18,... | collective-permute-start | bytes 393224 | tf_op jit(solution)/shard_map/ppermute | solution.py:281
  14.8 7.2 %collective-permute-start.1 = (f32[256,128]{1,0:T(8,128)S(1)}, f32[256,128]{1,0:T(8,128)S(1)}, u32[]{:S(2)}, u32[]{:S(2)}) collective-permute-start(f32[256,128]{1,0:T(8,128)S(1)} %get-tuple-element.66), channel_id=1, source_target_pairs={{0,2},{2,0},{4,6},{6,4},{8,10},{10,8},{12,14},{14,12},{16,18},{18,... | collective-permute-start | bytes 393224 | tf_op jit(solution)/shard_map/ppermute | solution.py:281
  16.0 13.0 %collective-permute-start.5 = (f32[512,128]{1,0:T(8,128)S(1)}, f32[512,128]{1,0:T(8,128)S(1)}, u32[]{:S(2)}, u32[]{:S(2)}) collective-permute-start(f32[512,128]{1,0:T(8,128)S(1)} %expand.8), channel_id=1, source_target_pairs={{0,4},{2,6},{4,0},{6,2},{8,12},{10,14},{12,8},{14,10},{16,20},{18,... | collective-permute-start | bytes 786440 | tf_op jit(solution)/shard_map/ppermute | solution.py:281
  20.4 6.9 %collective-permute-start.7 = (f32[512,128]{1,0:T(8,128)S(1)}, f32[512,128]{1,0:T(8,128)S(1)}, u32[]{:S(2)}, u32[]{:S(2)}) collective-permute-start(f32[512,128]{1,0:T(8,128)S(1)} %get-tuple-element.81), channel_id=1, source_target_pairs={{0,1},{1,0},{2,3},{3,2},{4,5},{5,4},{6,7},{7,6},{8,9},{9,8},{10,11... | collective-permute-start | bytes 786440 | tf_op jit(solution)/shard_map/ppermute | solution.py:281
  22.0 1.4 %collective-permute-start.6 = (f32[256,128]{1,0:T(8,128)S(1)}, f32[256,128]{1,0:T(8,128)S(1)}, u32[]{:S(2)}, u32[]{:S(2)}) collective-permute-start(f32[256,128]{1,0:T(8,128)S(1)} %get-tuple-element.77), channel_id=1, source_target_pairs={{0,2},{2,0},{4,6},{6,4},{8,10},{10,8},{12,14},{14,12},{16,18},{18,... | collective-permute-start | bytes 393224 | tf_op jit(solution)/shard_map/ppermute | solution.py:281
  22.1 6.3 %collective-permute-start.10 = (f32[256,128]{1,0:T(8,128)S(1)}, f32[256,128]{1,0:T(8,128)S(1)}, u32[]{:S(2)}, u32[]{:S(2)}) collective-permute-start(f32[256,128]{1,0:T(8,128)S(1)} %get-tuple-element.87), channel_id=1, source_target_pairs={{0,2},{2,0},{4,6},{6,4},{8,10},{10,8},{12,14},{14,12},{16,18},{18,... | collective-permute-start | bytes 393224 | tf_op jit(solution)/shard_map/ppermute | solution.py:281
  23.7 11.1 %collective-permute-start.16 = (f32[512,128]{1,0:T(8,128)S(1)}, f32[512,128]{1,0:T(8,128)S(1)}, u32[]{:S(2)}, u32[]{:S(2)}) collective-permute-start(f32[512,128]{1,0:T(8,128)S(1)} %expand.10), channel_id=1, source_target_pairs={{0,4},{2,6},{4,0},{6,2},{8,12},{10,14},{12,8},{14,10},{16,20},{18,... | collective-permute-start | bytes 786440 | tf_op jit(solution)/shard_map/ppermute | solution.py:281
  25.5 8.1 %collective-permute-start.11 = (f32[512,128]{1,0:T(8,128)S(1)}, f32[512,128]{1,0:T(8,128)S(1)}, u32[]{:S(2)}, u32[]{:S(2)}) collective-permute-start(f32[512,128]{1,0:T(8,128)S(1)} %get-tuple-element.92), channel_id=1, source_target_pairs={{0,1},{1,0},{2,3},{3,2},{4,5},{5,4},{6,7},{7,6},{8,9},{9,8},{10,11... | collective-permute-start | bytes 786440 | tf_op jit(solution)/shard_map/ppermute | solution.py:281
  28.4 2.5 %collective-permute-start.9 = (f32[256,128]{1,0:T(8,128)S(1)}, f32[256,128]{1,0:T(8,128)S(1)}, u32[]{:S(2)}, u32[]{:S(2)}) collective-permute-start(f32[256,128]{1,0:T(8,128)S(1)} %get-tuple-element.85), channel_id=1, source_target_pairs={{0,2},{2,0},{4,6},{6,4},{8,10},{10,8},{12,14},{14,12},{16,18},{18,... | collective-permute-start | bytes 393224 | tf_op jit(solution)/shard_map/ppermute | solution.py:281
  28.5 6.3 %collective-permute-start.15 = (f32[256,128]{1,0:T(8,128)S(1)}, f32[256,128]{1,0:T(8,128)S(1)}, u32[]{:S(2)}, u32[]{:S(2)}) collective-permute-start(f32[256,128]{1,0:T(8,128)S(1)} %get-tuple-element.100), channel_id=1, source_target_pairs={{0,2},{2,0},{4,6},{6,4},{8,10},{10,8},{12,14},{14,12},{16,18},{18,... | collective-permute-start | bytes 393224 | tf_op jit(solution)/shard_map/ppermute | solution.py:281
  29.0 8.0 %collective-permute-start.8 = (f32[256,128]{1,0:T(8,128)S(1)}, f32[256,128]{1,0:T(8,128)S(1)}, u32[]{:S(2)}, u32[]{:S(2)}) collective-permute-start(f32[256,128]{1,0:T(8,128)S(1)} %slice_add_fusion.3), channel_id=1, source_target_pairs={{0,8},{2,10},{4,12},{6,14},{8,0},{10,2},{12,4},{14,6},{16,24},{18,... | collective-permute-start | bytes 393224 | tf_op jit(solution)/shard_map/ppermute | solution.py:281
  31.2 12.0 %collective-permute-start.18 = (f32[512,128]{1,0:T(8,128)S(1)}, f32[512,128]{1,0:T(8,128)S(1)}, u32[]{:S(2)}, u32[]{:S(2)}) collective-permute-start(f32[512,128]{1,0:T(8,128)S(1)} %expand.12), channel_id=1, source_target_pairs={{0,4},{2,6},{4,0},{6,2},{8,12},{10,14},{12,8},{14,10},{16,20},{18,... | collective-permute-start | bytes 786440 | tf_op jit(solution)/shard_map/ppermute | solution.py:281
  34.8 6.2 %collective-permute-start.19 = (f32[256,128]{1,0:T(8,128)S(1)}, f32[256,128]{1,0:T(8,128)S(1)}, u32[]{:S(2)}, u32[]{:S(2)}) collective-permute-start(f32[256,128]{1,0:T(8,128)S(1)} %slice_add_fusion.2), channel_id=1, source_target_pairs={{0,8},{2,10},{4,12},{6,14},{8,0},{10,2},{12,4},{14,6},{16,24},{18,... | collective-permute-start | bytes 393224 | tf_op jit(solution)/shard_map/ppermute | solution.py:281
  36.5 4.5 %collective-permute-start.13 = (f32[256,128]{1,0:T(8,128)S(1)}, f32[256,128]{1,0:T(8,128)S(1)}, u32[]{:S(2)}, u32[]{:S(2)}) collective-permute-start(f32[256,128]{1,0:T(8,128)S(1)} %get-tuple-element.97), channel_id=1, source_target_pairs={{0,2},{2,0},{4,6},{6,4},{8,10},{10,8},{12,14},{14,12},{16,18},{18,... | collective-permute-start | bytes 393224 | tf_op jit(solution)/shard_map/ppermute | solution.py:281
  36.5 3.4 %collective-permute-start.14 = (f32[256,128]{1,0:T(8,128)S(1)}, f32[256,128]{1,0:T(8,128)S(1)}, u32[]{:S(2)}, u32[]{:S(2)}) collective-permute-start(f32[256,128]{1,0:T(8,128)S(1)} %get-tuple-element.98), channel_id=1, source_target_pairs={{0,2},{2,0},{4,6},{6,4},{8,10},{10,8},{12,14},{14,12},{16,18},{18,... | collective-permute-start | bytes 393224 | tf_op jit(solution)/shard_map/ppermute | solution.py:281
  37.0 14.1 %collective-permute-start.12 = (f32[128,128]{1,0:T(8,128)S(1)}, f32[128,128]{1,0:T(8,128)S(1)}, u32[]{:S(2)}, u32[]{:S(2)}) collective-permute-start(f32[128,128]{1,0:T(8,128)S(1)} %fusion.9), channel_id=1, source_target_pairs={{0,16},{2,18},{4,20},{6,22},{8,24},{10,26},{12,28},{14,30},{16,0},... | collective-permute-start | bytes 196616 | tf_op jit(solution)/shard_map/ppermute | solution.py:281
  40.1 9.3 %collective-permute-start.17 = (f32[512,128]{1,0:T(8,128)S(1)}, f32[512,128]{1,0:T(8,128)S(1)}, u32[]{:S(2)}, u32[]{:S(2)}) collective-permute-start(f32[512,128]{1,0:T(8,128)S(1)} %expand.14), channel_id=1, source_target_pairs={{0,4},{2,6},{4,0},{6,2},{8,12},{10,14},{12,8},{14,10},{16,20},{18,... | collective-permute-start | bytes 786440 | tf_op jit(solution)/shard_map/ppermute | solution.py:281
  41.0 10.0 %collective-permute-start.21 = (f32[128,128]{1,0:T(8,128)S(1)}, f32[128,128]{1,0:T(8,128)S(1)}, u32[]{:S(2)}, u32[]{:S(2)}) collective-permute-start(f32[128,128]{1,0:T(8,128)S(1)} %fusion.8), channel_id=1, source_target_pairs={{0,16},{2,18},{4,20},{6,22},{8,24},{10,26},{12,28},{14,30},{16,0},... | collective-permute-start | bytes 196616 | tf_op jit(solution)/shard_map/ppermute | solution.py:281
  43.2 5.2 %collective-permute-start.20 = (f32[256,128]{1,0:T(8,128)S(1)}, f32[256,128]{1,0:T(8,128)S(1)}, u32[]{:S(2)}, u32[]{:S(2)}) collective-permute-start(f32[256,128]{1,0:T(8,128)S(1)} %slice_add_fusion), channel_id=1, source_target_pairs={{0,8},{2,10},{4,12},{6,14},{8,0},{10,2},{12,4},{14,6},{16,24},{18,... | collective-permute-start | bytes 393224 | tf_op jit(solution)/shard_map/ppermute | solution.py:281
  48.4 5.3 %collective-permute-start.22 = (f32[128,128]{1,0:T(8,128)S(1)}, f32[128,128]{1,0:T(8,128)S(1)}, u32[]{:S(2)}, u32[]{:S(2)}) collective-permute-start(f32[128,128]{1,0:T(8,128)S(1)} %fusion.7), channel_id=1, source_target_pairs={{0,16},{2,18},{4,20},{6,22},{8,24},{10,26},{12,28},{14,30},{16,0},... | collective-permute-start | bytes 196616 | tf_op jit(solution)/shard_map/ppermute | solution.py:281
  49.5 5.6 %collective-permute-start.23 = (f32[256,128]{1,0:T(8,128)S(1)}, f32[256,128]{1,0:T(8,128)S(1)}, u32[]{:S(2)}, u32[]{:S(2)}) collective-permute-start(f32[256,128]{1,0:T(8,128)S(1)} %slice_add_fusion.1), channel_id=1, source_target_pairs={{0,8},{2,10},{4,12},{6,14},{8,0},{10,2},{12,4},{14,6},{16,24},{18,... | collective-permute-start | bytes 393224 | tf_op jit(solution)/shard_map/ppermute | solution.py:281
  55.1 5.9 %collective-permute-start.24 = (f32[128,128]{1,0:T(8,128)S(1)}, f32[128,128]{1,0:T(8,128)S(1)}, u32[]{:S(2)}, u32[]{:S(2)}) collective-permute-start(f32[128,128]{1,0:T(8,128)S(1)} %fusion), channel_id=1, source_target_pairs={{0,16},{2,18},{4,20},{6,22},{8,24},{10,26},{12,28},{14,30},{16,0},... | collective-permute-start | bytes 196616 | tf_op jit(solution)/shard_map/ppermute | solution.py:281
where the time goes:
time: 61.9 us; the launch traced here: 61.7 us
  starting transfers between devices  28.4 us (46%)
  Pallas kernels  16.6 us (27%)
  waiting for transfers between devices  15.6 us (25%)
  other arithmetic  0.9 us (1%)
    ppermute x25, starting transfers between devices, swap(): return lax.ppermute(x, axis, [(i, i ^ mask) for i in range(size)])  28.4 us
    ppermute x25, waiting for transfers between devices, swap(): return lax.ppermute(x, axis, [(i, i ^ mask) for i in range(size)])  15.6 us
    pallas_call x2, Pallas kernels, column_side(): pl.pallas_call(functools.partial(column_kernel, n_seg, pieces, start * CH...  9.5 us
    pallas_call x4, Pallas kernels, row_side(): pl.pallas_call(functools.partial(row_kernel, n_seg, n_tile, leaf), in_spe...  4.72 us
    pallas_call x8, Pallas kernels, expanded(): pl.pallas_call(functools.partial(expand_kernel, part), in_specs=[in_vmem]...  1.89 us
  transfers between devices with their start and end apart: 25, of which 9 were waited for; matrix products, arithmetic and copies ran while one was open for 0% of the time, Pallas kernels for 21%

commit v1 on v0

--- a/solution.py
+++ b/solution.py
@@ -10,6 +10,8 @@
 F32 = jnp.float32
 BF16 = jnp.bfloat16
 CHUNK = 128
+FIRST = 52.5
+SECOND = 52
 
 
 def split(x):
@@ -226,7 +228,7 @@
                 pltpu.VMEM((box * rank, width), BF16),
                 pltpu.SemaphoreType.DMA((2 * pieces + 2 * levels + 1,)),
             ],
-            compiler_params=pltpu.CompilerParams(vmem_limit_bytes=limit * 2**20),
+            compiler_params=pltpu.CompilerParams(vmem_limit_bytes=int(limit * 2**20)),
             cost_estimate=cost,
             name="column_side",
         )(right_sides, proj, col, mid)
@@ -290,9 +292,9 @@
         left = terms[-1].shape[0]
         return total(terms, left // 2, left)
 
-    parts = column_side(0, 1, mid, 53)
+    parts = column_side(0, 2, mid, FIRST)
     received = {0: exchange(parts[0])}
-    parts += column_side(1, chunks - 1, tie(mid, parts[0][-1]), 52)
+    parts += column_side(2, chunks - 2, tie(mid, parts[0][-1]), SECOND)
     received[1] = exchange(parts[1])
     wide = row_weights()
     last_wide = expand_weights(swap(tie(expand, parts[-1][0]), "tile", n_tile, 1))
@@ -300,17 +302,23 @@
     terms, sends, lows = [], {}, []
     last = chunks - 1
 
-    def forward(c, b, *after):
-        terms[c][-1] = tie(terms[c][-1], *after)
-        sends[c, b] = next_send(terms[c])
-        terms[c].append(swap(sends[c, b], "tile", n_tile, 1 << b))
-        return sends[c, b]
+    def forward(group, b, *after):
+        for c in group:
+            terms[c][-1] = tie(terms[c][-1], *after)
+        send = jnp.concatenate([next_send(terms[c]) for c in group])
+        sends[group[-1], b] = send
+        got = swap(send, "tile", n_tile, 1 << b)
+        rows = got.shape[0] // len(group)
+        for k, c in enumerate(group):
+            terms[c].append(got[k * rows:(k + 1) * rows])
+        return send
 
     def low_half(c, *after):
         own, other = lows[c]
         terms[c][0] = expanded(0, own, tie(other, *after), last_wide)
         return terms[c][0]
 
+    early = list(range(last - 1))
     for c in range(chunks):
         after = sends[c - 1, 1] if c else parts[-1][0]
         own_low, own_high, low, high = row_side([tie(x, after) for x in received[c]], wide)
@@ -318,10 +326,8 @@
         done = []
         if c >= 1:
             done.append(low_half(c - 1, own_high))
-        if c >= 2:
-            done.append(forward(c - 2, 2, own_high))
-        if c >= 3 and bits > 3:
-            done.append(forward(c - 3, 3, own_high))
+        if c == last:
+            done.append(forward(early, 2, own_high))
         got = swap(high, "tile", n_tile, 1)
         if done:
             got = tie(got, *done)
@@ -330,14 +336,14 @@
         if c + 2 < chunks:
             received[c + 2] = exchange(parts[c + 2], sends[c, 1])
     low_half(last, sends[last, 1])
-    done = [forward(last - 1, 2, sends[last, 1])]
+    done = [forward([last - 1], 2, sends[last, 1])]
     if bits > 3:
-        done += [forward(k, 3, sends[last, 1]) for k in range(max(0, last - 2), last)]
-    forward(last, 2, *done)
+        done += [forward(group, 3, sends[last, 1]) for group in (early, [last - 1])]
+    forward([last], 2, *done)
     for b in range(3, bits):
-        for c in range(chunks):
-            if (c, b) not in sends:
-                forward(c, b, sends[last, 2])
+        for group in (early, [last - 1], [last]):
+            if (group[-1], b) not in sends:
+                forward(group, b, sends[last, 2])
     for c in range(last):
         terms[c][-1] = tie(terms[c][-1], sends[last, 2])
     return jnp.concatenate([total(t, 0, out_rows) for t in terms], axis=1)

time: 61.9 us -> 64.9 us (1.048)
  waiting for transfers between devices: 15.6 us -> 20.5 us
  starting transfers between devices: 28.4 us -> 26.5 us
    ppermute x25 -> x23, waiting for transfers between devices: 15.6 us -> 20.5 us  [swap(): return lax.ppermute(x, axis, [(i, i ^ mask) for i in range(size)])]
    ppermute x25 -> x23, starting transfers between devices: 28.4 us -> 26.5 us  [swap(): return lax.ppermute(x, axis, [(i, i ^ mask) for i in range(size)])]
  transfers between devices with their start and end apart: 25 -> 23, of which waited for: 9 -> 12; matrix products, arithmetic and copies ran while one was open for 0% -> 0% of each run, Pallas kernels for 21% -> 18%
where the time goes in v1:
time: 64.9 us; the launch traced here: 64.7 us
  starting transfers between devices  26.5 us (41%)
  waiting for transfers between devices  20.5 us (32%)
  Pallas kernels  16.4 us (25%)
  other arithmetic  0.94 us (1%)
    ppermute x23, starting transfers between devices, swap(): return lax.ppermute(x, axis, [(i, i ^ mask) for i in range(size)])  26.5 us
    ppermute x23, waiting for transfers between devices, swap(): return lax.ppermute(x, axis, [(i, i ^ mask) for i in range(size)])  20.5 us
    pallas_call x2, Pallas kernels, column_side(): pl.pallas_call(functools.partial(column_kernel, n_seg, pieces, start * CH...  9.36 us
    pallas_call x4, Pallas kernels, row_side(): pl.pallas_call(functools.partial(row_kernel, n_seg, n_tile, leaf), in_spe...  4.71 us
    pallas_call x8, Pallas kernels, expanded(): pl.pallas_call(functools.partial(expand_kernel, part), in_specs=[in_vmem]...  1.89 us
  transfers between devices with their start and end apart: 23, of which 12 were waited for; matrix products, arithmetic and copies ran while one was open for 0% of the time, Pallas kernels for 18%

profile of v1, /device:TPU:0, one launch (start us, length us, event | category | flops | bytes accessed | tf_op | source)
XLA Modules:
  0.0 64.7 jit_solution(18421319268337142147)
XLA Ops:
  0.0 4.7 %column_side.2 = (f32[512,128]{1,0:T(8,128)S(1)}, f32[512,128]{1,0:T(8,128)S(1)}, f32[512,128]{1,0:T(8,128)S(1)}, f32[512,128]{1,0:T(8,128)S(1)}) custom-call(f32[2048,512]{1,0:T(8,128)} %x_hbm.3, f32[16,64,128]{2,1,0:T(8,128)} %bitcast.7, f32[4,8,128,128]{3,2,1,0:T(8,128)} %bitcast.12, f32[16,64,64]{2,1,0:T(8,128)} %bitcast.14), custom_call_target="tpu_custom_call" | custom-call | flops 1000000 | bytes 100000 | tf_op jit(solution)/shard_map/column_side/pallas_call | solution.py:217
  4.7 0.0 copy-start.2
  4.7 0.0 copy-start.1
  4.7 3.0 %collective-permute-start = (f32[512,128]{1,0:T(8,128)S(1)}, f32[512,128]{1,0:T(8,128)S(1)}, u32[]{:S(2)}, u32[]{:S(2)}) collective-permute-start(f32[512,128]{1,0:T(8,128)S(1)} %get-tuple-element.60), channel_id=1, source_target_pairs={{0,1},{1,0},{2,3},{3,2},{4,5},{5,4},{6,7},{7,6},{8,9},{9,8},{10,11... | collective-permute-start | bytes 786440 | tf_op jit(solution)/shard_map/ppermute | solution.py:283
  7.7 4.7 %column_side.3 = (f32[512,128]{1,0:T(8,128)S(1)}, f32[512,128]{1,0:T(8,128)S(1)}, f32[512,128]{1,0:T(8,128)S(1)}, f32[512,128]{1,0:T(8,128)S(1)}) custom-call(f32[2048,512]{1,0:T(8,128)} %x_hbm.3, f32[16,64,128]{2,1,0:T(8,128)S(1)} %bitcast.8, f32[4,8,128,128]{3,2,1,0:T(8,128)} %bitcast.13, f32[16,64,64]{2,1,0:T(8,128)} %bitcast.15), custom_call_target="tpu_custom_call" | custom-call | flops 1000000 | bytes 100000 | tf_op jit(solution)/shard_map/column_side/pallas_call | solution.py:217
  12.4 0.1 collective-permute-start.3
  12.5 0.5 collective-permute-start.4
  13.0 0.3 row_weights.1.refs_2_
  13.3 0.7 %collective-permute-done.refs_1_ = f32[512,128]{1,0:T(8,128)S(1)} collective-permute-done((f32[512,128]{1,0:T(8,128)S(1)}, f32[512,128]{1,0:T(8,128)S(1)}, u32[]{:S(2)}, u32[]{:S(2)}) %collective-permute-start) | collective-permute-done | bytes 262176 | tf_op jit(solution)/shard_map/ppermute | solution.py:283
  14.0 1.2 %row_side.4 = (f32[256,128]{1,0:T(8,128)S(1)}, f32[256,128]{1,0:T(8,128)S(1)}, f32[256,128]{1,0:T(8,128)S(1)}, f32[256,128]{1,0:T(8,128)S(1)}) custom-call(f32[512,128]{1,0:T(8,128)S(1)} %get-tuple-element.63.refs_0_, f32[512,128]{1,0:T(8,128)S(1)} %collective-permute-done.refs_1_, bf16[4,8,128,256]{3,2,1,0:T(8,128)(2,1)S(1)} %row_weights.1.refs_2_), custom_call_target="tpu_custom_call" | custom-call | flops 20000000000 | bytes 100000 | tf_op jit(solution)/shard_map/row_side/pallas_call | solution.py:260
  15.2 0.1 collective-permute-start.2
  15.3 0.5 collective-permute-start.1
  15.8 0.0 collective-permute-done.3.other_ref
  15.8 0.2 expand_weights.1.last_ref
  16.0 0.6 collective-permute-done.2.other_ref
  16.6 0.2 expand.8
  16.8 1.8 %collective-permute-start.5 = (f32[512,128]{1,0:T(8,128)S(1)}, f32[512,128]{1,0:T(8,128)S(1)}, u32[]{:S(2)}, u32[]{:S(2)}) collective-permute-start(f32[512,128]{1,0:T(8,128)S(1)} %expand.8), channel_id=1, source_target_pairs={{0,4},{2,6},{4,0},{6,2},{8,12},{10,14},{12,8},{14,10},{16,20},{18,... | collective-permute-start | bytes 786440 | tf_op jit(solution)/shard_map/ppermute | solution.py:283
  18.7 2.5 %collective-permute-done.4.refs_1_ = f32[512,128]{1,0:T(8,128)S(1)} collective-permute-done((f32[512,128]{1,0:T(8,128)S(1)}, f32[512,128]{1,0:T(8,128)S(1)}, u32[]{:S(2)}, u32[]{:S(2)}) %collective-permute-start.4) | collective-permute-done | bytes 262176 | tf_op jit(solution)/shard_map/ppermute | solution.py:283
  21.2 0.5 collective-permute-start.7
  21.7 1.2 %row_side.5 = (f32[256,128]{1,0:T(8,128)S(1)}, f32[256,128]{1,0:T(8,128)S(1)}, f32[256,128]{1,0:T(8,128)S(1)}, f32[256,128]{1,0:T(8,128)S(1)}) custom-call(f32[512,128]{1,0:T(8,128)S(1)} %get-tuple-element.71.refs_0_, f32[512,128]{1,0:T(8,128)S(1)} %collective-permute-done.4.refs_1_, bf16[4,8,128,256]{3,2,1,0:T(8,128)(2,1)S(1)} %row_weights.1.refs_2_), custom_call_target="tpu_custom_call" | custom-call | flops 20000000000 | bytes 100000 | tf_op jit(solution)/shard_map/row_side/pallas_call | solution.py:260
  22.8 0.0 collective-permute-done.1.other_ref
  22.9 0.1 collective-permute-start.6
  22.9 0.5 collective-permute-start.9
  23.4 0.2 expand.9
  23.7 0.6 collective-permute-done.6.other_ref
  24.3 0.2 expand.10
  24.5 1.7 %collective-permute-start.11 = (f32[512,128]{1,0:T(8,128)S(1)}, f32[512,128]{1,0:T(8,128)S(1)}, u32[]{:S(2)}, u32[]{:S(2)}) collective-permute-start(f32[512,128]{1,0:T(8,128)S(1)} %expand.10), channel_id=1, source_target_pairs={{0,4},{2,6},{4,0},{6,2},{8,12},{10,14},{12,8},{14,10},{16,20},{18,... | collective-permute-start | bytes 786440 | tf_op jit(solution)/shard_map/ppermute | solution.py:283
  26.2 1.5 %collective-permute-start.10 = (f32[512,128]{1,0:T(8,128)S(1)}, f32[512,128]{1,0:T(8,128)S(1)}, u32[]{:S(2)}, u32[]{:S(2)}) collective-permute-start(f32[512,128]{1,0:T(8,128)S(1)} %get-tuple-element.91), channel_id=1, source_target_pairs={{0,1},{1,0},{2,3},{3,2},{4,5},{5,4},{6,7},{7,6},{8,9},{9,8},{10,11... | collective-permute-start | bytes 786440 | tf_op jit(solution)/shard_map/ppermute | solution.py:283
  27.7 1.7 %collective-permute-done.7.refs_1_ = f32[512,128]{1,0:T(8,128)S(1)} collective-permute-done((f32[512,128]{1,0:T(8,128)S(1)}, f32[512,128]{1,0:T(8,128)S(1)}, u32[]{:S(2)}, u32[]{:S(2)}) %collective-permute-start.7) | collective-permute-done | bytes 262176 | tf_op jit(solution)/shard_map/ppermute | solution.py:283
  29.4 1.2 %row_side.6 = (f32[256,128]{1,0:T(8,128)S(1)}, f32[256,128]{1,0:T(8,128)S(1)}, f32[256,128]{1,0:T(8,128)S(1)}, f32[256,128]{1,0:T(8,128)S(1)}) custom-call(f32[512,128]{1,0:T(8,128)S(1)} %get-tuple-element.79.refs_0_, f32[512,128]{1,0:T(8,128)S(1)} %collective-permute-done.7.refs_1_, bf16[4,8,128,256]{3,2,1,0:T(8,128)(2,1)S(1)} %row_weights.1.refs_2_), custom_call_target="tpu_custom_call" | custom-call | flops 20000000000 | bytes 100000 | tf_op jit(solution)/shard_map/row_side/pallas_call | solution.py:260
  30.6 0.0 collective-permute-done.9.other_ref
  30.6 0.1 collective-permute-start.8
  30.7 0.5 collective-permute-start.14
  31.2 0.2 expand.11
  31.4 0.6 collective-permute-done.8.other_ref
  32.0 0.2 expand.12
  32.3 2.6 %collective-permute-start.18 = (f32[512,128]{1,0:T(8,128)S(1)}, f32[512,128]{1,0:T(8,128)S(1)}, u32[]{:S(2)}, u32[]{:S(2)}) collective-permute-start(f32[512,128]{1,0:T(8,128)S(1)} %expand.12), channel_id=1, source_target_pairs={{0,4},{2,6},{4,0},{6,2},{8,12},{10,14},{12,8},{14,10},{16,20},{18,... | collective-permute-start | bytes 786440 | tf_op jit(solution)/shard_map/ppermute | solution.py:283
  34.9 0.0 collective-permute-done.10.refs_1_
  34.9 1.2 %row_side.7 = (f32[256,128]{1,0:T(8,128)S(1)}, f32[256,128]{1,0:T(8,128)S(1)}, f32[256,128]{1,0:T(8,128)S(1)}, f32[256,128]{1,0:T(8,128)S(1)}) custom-call(f32[512,128]{1,0:T(8,128)S(1)} %get-tuple-element.89.refs_0_, f32[512,128]{1,0:T(8,128)S(1)} %collective-permute-done.10.refs_1_, bf16[4,8,128,256]{3,2,1,0:T(8,128)(2,1)S(1)} %row_weights.1.refs_2_), custom_call_target="tpu_custom_call" | custom-call | flops 20000000000 | bytes 100000 | tf_op jit(solution)/shard_map/row_side/pallas_call | solution.py:260
  36.1 0.0 collective-permute-done.5
  36.1 0.0 collective-permute-done.11
  36.1 0.0 collective-permute-done.14.other_ref
  36.2 0.1 collective-permute-start.13
  36.3 1.6 %collective-permute-start.12 = (f32[512,128]{1,0:T(8,128)S(1)}, f32[512,128]{1,0:T(8,128)S(1)}, u32[]{:S(2)}, u32[]{:S(2)}) collective-permute-start(f32[512,128]{1,0:T(8,128)S(1)} %pad_maximum_fusion), channel_id=1, source_target_pairs={{0,8},{2,10},{4,12},{6,14},{8,0},{10,2},{12,4},{14,6},{16,24},{18,... | collective-permute-start | bytes 786440 | tf_op jit(solution)/shard_map/ppermute | solution.py:283
  37.9 0.2 collective-permute-start.16
  38.1 0.2 expand.13
  38.3 0.0 collective-permute-done.13.other_ref
  38.3 0.2 expand.14
  38.6 1.4 %collective-permute-start.17 = (f32[512,128]{1,0:T(8,128)S(1)}, f32[512,128]{1,0:T(8,128)S(1)}, u32[]{:S(2)}, u32[]{:S(2)}) collective-permute-start(f32[512,128]{1,0:T(8,128)S(1)} %expand.14), channel_id=1, source_target_pairs={{0,4},{2,6},{4,0},{6,2},{8,12},{10,14},{12,8},{14,10},{16,20},{18,... | collective-permute-start | bytes 786440 | tf_op jit(solution)/shard_map/ppermute | solution.py:283
  40.0 0.0 collective-permute-done.16.other_ref
  40.0 0.2 expand.15
  40.2 1.3 %collective-permute-done.18 = f32[512,128]{1,0:T(8,128)S(1)} collective-permute-done((f32[512,128]{1,0:T(8,128)S(1)}, f32[512,128]{1,0:T(8,128)S(1)}, u32[]{:S(2)}, u32[]{:S(2)}) %collective-permute-start.18) | collective-permute-done | bytes 262176 | tf_op jit(solution)/shard_map/ppermute | solution.py:283
  41.5 2.1 %collective-permute-start.19 = (f32[256,128]{1,0:T(8,128)S(1)}, f32[256,128]{1,0:T(8,128)S(1)}, u32[]{:S(2)}, u32[]{:S(2)}) collective-permute-start(f32[256,128]{1,0:T(8,128)S(1)} %slice_add_fusion), channel_id=1, source_target_pairs={{0,8},{2,10},{4,12},{6,14},{8,0},{10,2},{12,4},{14,6},{16,24},{18,... | collective-permute-start | bytes 393224 | tf_op jit(solution)/shard_map/ppermute | solution.py:283
  43.6 1.8 %collective-permute-done.12 = f32[512,128]{1,0:T(8,128)S(1)} collective-permute-done((f32[512,128]{1,0:T(8,128)S(1)}, f32[512,128]{1,0:T(8,128)S(1)}, u32[]{:S(2)}, u32[]{:S(2)}) %collective-permute-start.12) | collective-permute-done | bytes 262176 | tf_op jit(solution)/shard_map/ppermute | solution.py:283
  45.5 2.7 %collective-permute-start.15 = (f32[256,128]{1,0:T(8,128)S(1)}, f32[256,128]{1,0:T(8,128)S(1)}, u32[]{:S(2)}, u32[]{:S(2)}) collective-permute-start(f32[256,128]{1,0:T(8,128)S(1)} %pad_maximum_fusion.2), channel_id=1, source_target_pairs={{0,16},{2,18},{4,20},{6,22},{8,24},{10,26},{12,28},{14,30},{16,0},... | collective-permute-start | bytes 393224 | tf_op jit(solution)/shard_map/ppermute | solution.py:283
  48.2 2.7 %collective-permute-start.20 = (f32[128,128]{1,0:T(8,128)S(1)}, f32[128,128]{1,0:T(8,128)S(1)}, u32[]{:S(2)}, u32[]{:S(2)}) collective-permute-start(f32[128,128]{1,0:T(8,128)S(1)} %fusion.7), channel_id=1, source_target_pairs={{0,16},{2,18},{4,20},{6,22},{8,24},{10,26},{12,28},{14,30},{16,0},... | collective-permute-start | bytes 196616 | tf_op jit(solution)/shard_map/ppermute | solution.py:283
  50.9 0.0 collective-permute-done.17
  50.9 1.2 %collective-permute-start.21 = (f32[256,128]{1,0:T(8,128)S(1)}, f32[256,128]{1,0:T(8,128)S(1)}, u32[]{:S(2)}, u32[]{:S(2)}) collective-permute-start(f32[256,128]{1,0:T(8,128)S(1)} %slice_add_fusion.1), channel_id=1, source_target_pairs={{0,8},{2,10},{4,12},{6,14},{8,0},{10,2},{12,4},{14,6},{16,24},{18,... | collective-permute-start | bytes 393224 | tf_op jit(solution)/shard_map/ppermute | solution.py:283
  52.2 4.0 %collective-permute-done.15 = f32[256,128]{1,0:T(8,128)S(1)} collective-permute-done((f32[256,128]{1,0:T(8,128)S(1)}, f32[256,128]{1,0:T(8,128)S(1)}, u32[]{:S(2)}, u32[]{:S(2)}) %collective-permute-start.15) | collective-permute-done | bytes 131104 | tf_op jit(solution)/shard_map/ppermute | solution.py:283
  56.2 0.6 collective-permute-done.20
  56.9 1.2 %collective-permute-done.21 = f32[256,128]{1,0:T(8,128)S(1)} collective-permute-done((f32[256,128]{1,0:T(8,128)S(1)}, f32[256,128]{1,0:T(8,128)S(1)}, u32[]{:S(2)}, u32[]{:S(2)}) %collective-permute-start.21) | collective-permute-done | bytes 131104 | tf_op jit(solution)/shard_map/ppermute | solution.py:283
  58.1 1.1 %collective-permute-start.22 = (f32[128,128]{1,0:T(8,128)S(1)}, f32[128,128]{1,0:T(8,128)S(1)}, u32[]{:S(2)}, u32[]{:S(2)}) collective-permute-start(f32[128,128]{1,0:T(8,128)S(1)} %fusion), channel_id=1, source_target_pairs={{0,16},{2,18},{4,20},{6,22},{8,24},{10,26},{12,28},{14,30},{16,0},... | collective-permute-start | bytes 196616 | tf_op jit(solution)/shard_map/ppermute | solution.py:283
  59.2 4.8 %collective-permute-done.22 = f32[128,128]{1,0:T(8,128)S(1)} collective-permute-done((f32[128,128]{1,0:T(8,128)S(1)}, f32[128,128]{1,0:T(8,128)S(1)}, u32[]{:S(2)}, u32[]{:S(2)}) %collective-permute-start.22) | collective-permute-done | bytes 65568 | tf_op jit(solution)/shard_map/ppermute | solution.py:283
  64.0 0.7 %pad_maximum_fusion.1 = f32[128,512]{1,0:T(8,128)} fusion(f32[128,128]{1,0:T(8,128)S(1)} %fusion.2, f32[128,128]{1,0:T(8,128)S(1)} %fusion.4, f32[128,128]{1,0:T(8,128)S(1)} %fusion.6, f32[128,128]{1,0:T(8,128)S(1)} %fusion.11), kind=kLoop, calls=%fused_computation.1 | loop fusion | flops 196608 | bytes 524288 | tf_op jit(solution)/shard_map/concatenate | solution.py:349
  (20 shorter events, 0.3 us)
Async XLA Ops:
  0.0 7.7 %copy-start = (f32[1,16,64,128]{3,2,1,0:T(8,128)S(1)}, f32[1,16,64,128]{3,2,1,0:T(8,128)}, u32[]{:S(2)}) copy-start(f32[1,16,64,128]{3,2,1,0:T(8,128)} %param.7) | copy-start | bytes 1572868
  4.7 7.7 %copy-start.2 = (f32[1,16,128,64]{2,3,1,0:T(8,128)S(1)}, f32[1,16,128,64]{2,3,1,0:T(8,128)}, u32[]{:S(2)}) copy-start(f32[1,16,128,64]{2,3,1,0:T(8,128)} %param.11) | copy-start | bytes 1572868
  4.7 8.3 %copy-start.1 = (f32[1,4,8,128,128]{4,3,2,1,0:T(8,128)S(1)}, f32[1,4,8,128,128]{4,3,2,1,0:T(8,128)}, u32[]{:S(2)}) copy-start(f32[1,4,8,128,128]{4,3,2,1,0:T(8,128)} %param.10) | copy-start | bytes 6291460
  4.7 9.3 %collective-permute-start = (f32[512,128]{1,0:T(8,128)S(1)}, f32[512,128]{1,0:T(8,128)S(1)}, u32[]{:S(2)}, u32[]{:S(2)}) collective-permute-start(f32[512,128]{1,0:T(8,128)S(1)} %get-tuple-element.60), channel_id=1, source_target_pairs={{0,1},{1,0},{2,3},{3,2},{4,5},{5,4},{6,7},{7,6},{8,9},{9,8},{10,11... | collective-permute-start | bytes 786440 | tf_op jit(solution)/shard_map/ppermute | solution.py:283
  12.4 3.4 %collective-permute-start.3 = (f32[16,64,128]{2,1,0:T(8,128)S(1)}, f32[16,64,128]{2,1,0:T(8,128)S(1)}, u32[]{:S(2)}, u32[]{:S(2)}) collective-permute-start(f32[16,64,128]{2,1,0:T(8,128)S(1)} %bitcast.10), channel_id=1, source_target_pairs={{0,2},{2,0},{4,6},{6,4},{8,10},{10,8},{12,14},{14,12},{16,18},{18,... | collective-permute-start | bytes 1572872 | tf_op jit(solution)/shard_map/ppermute | solution.py:283
  12.5 8.7 %collective-permute-start.4 = (f32[512,128]{1,0:T(8,128)S(1)}, f32[512,128]{1,0:T(8,128)S(1)}, u32[]{:S(2)}, u32[]{:S(2)}) collective-permute-start(f32[512,128]{1,0:T(8,128)S(1)} %get-tuple-element.72), channel_id=1, source_target_pairs={{0,1},{1,0},{2,3},{3,2},{4,5},{5,4},{6,7},{7,6},{8,9},{9,8},{10,11... | collective-permute-start | bytes 786440 | tf_op jit(solution)/shard_map/ppermute | solution.py:283
  15.2 1.4 %collective-permute-start.2 = (f32[256,128]{1,0:T(8,128)S(1)}, f32[256,128]{1,0:T(8,128)S(1)}, u32[]{:S(2)}, u32[]{:S(2)}) collective-permute-start(f32[256,128]{1,0:T(8,128)S(1)} %get-tuple-element.69), channel_id=1, source_target_pairs={{0,2},{2,0},{4,6},{6,4},{8,10},{10,8},{12,14},{14,12},{16,18},{18,... | collective-permute-start | bytes 393224 | tf_op jit(solution)/shard_map/ppermute | solution.py:283
  15.3 7.6 %collective-permute-start.1 = (f32[256,128]{1,0:T(8,128)S(1)}, f32[256,128]{1,0:T(8,128)S(1)}, u32[]{:S(2)}, u32[]{:S(2)}) collective-permute-start(f32[256,128]{1,0:T(8,128)S(1)} %get-tuple-element.66), channel_id=1, source_target_pairs={{0,2},{2,0},{4,6},{6,4},{8,10},{10,8},{12,14},{14,12},{16,18},{18,... | collective-permute-start | bytes 393224 | tf_op jit(solution)/shard_map/ppermute | solution.py:283
  16.8 19.2 %collective-permute-start.5 = (f32[512,128]{1,0:T(8,128)S(1)}, f32[512,128]{1,0:T(8,128)S(1)}, u32[]{:S(2)}, u32[]{:S(2)}) collective-permute-start(f32[512,128]{1,0:T(8,128)S(1)} %expand.8), channel_id=1, source_target_pairs={{0,4},{2,6},{4,0},{6,2},{8,12},{10,14},{12,8},{14,10},{16,20},{18,... | collective-permute-start | bytes 786440 | tf_op jit(solution)/shard_map/ppermute | solution.py:283
  21.2 8.2 %collective-permute-start.7 = (f32[512,128]{1,0:T(8,128)S(1)}, f32[512,128]{1,0:T(8,128)S(1)}, u32[]{:S(2)}, u32[]{:S(2)}) collective-permute-start(f32[512,128]{1,0:T(8,128)S(1)} %get-tuple-element.81), channel_id=1, source_target_pairs={{0,1},{1,0},{2,3},{3,2},{4,5},{5,4},{6,7},{7,6},{8,9},{9,8},{10,11... | collective-permute-start | bytes 786440 | tf_op jit(solution)/shard_map/ppermute | solution.py:283
  22.9 1.4 %collective-permute-start.6 = (f32[256,128]{1,0:T(8,128)S(1)}, f32[256,128]{1,0:T(8,128)S(1)}, u32[]{:S(2)}, u32[]{:S(2)}) collective-permute-start(f32[256,128]{1,0:T(8,128)S(1)} %get-tuple-element.77), channel_id=1, source_target_pairs={{0,2},{2,0},{4,6},{6,4},{8,10},{10,8},{12,14},{14,12},{16,18},{18,... | collective-permute-start | bytes 393224 | tf_op jit(solution)/shard_map/ppermute | solution.py:283
  22.9 7.7 %collective-permute-start.9 = (f32[256,128]{1,0:T(8,128)S(1)}, f32[256,128]{1,0:T(8,128)S(1)}, u32[]{:S(2)}, u32[]{:S(2)}) collective-permute-start(f32[256,128]{1,0:T(8,128)S(1)} %get-tuple-element.86), channel_id=1, source_target_pairs={{0,2},{2,0},{4,6},{6,4},{8,10},{10,8},{12,14},{14,12},{16,18},{18,... | collective-permute-start | bytes 393224 | tf_op jit(solution)/shard_map/ppermute | solution.py:283
  24.5 11.6 %collective-permute-start.11 = (f32[512,128]{1,0:T(8,128)S(1)}, f32[512,128]{1,0:T(8,128)S(1)}, u32[]{:S(2)}, u32[]{:S(2)}) collective-permute-start(f32[512,128]{1,0:T(8,128)S(1)} %expand.10), channel_id=1, source_target_pairs={{0,4},{2,6},{4,0},{6,2},{8,12},{10,14},{12,8},{14,10},{16,20},{18,... | collective-permute-start | bytes 786440 | tf_op jit(solution)/shard_map/ppermute | solution.py:283
  26.2 8.7 %collective-permute-start.10 = (f32[512,128]{1,0:T(8,128)S(1)}, f32[512,128]{1,0:T(8,128)S(1)}, u32[]{:S(2)}, u32[]{:S(2)}) collective-permute-start(f32[512,128]{1,0:T(8,128)S(1)} %get-tuple-element.91), channel_id=1, source_target_pairs={{0,1},{1,0},{2,3},{3,2},{4,5},{5,4},{6,7},{7,6},{8,9},{9,8},{10,11... | collective-permute-start | bytes 786440 | tf_op jit(solution)/shard_map/ppermute | solution.py:283
  30.6 1.4 %collective-permute-start.8 = (f32[256,128]{1,0:T(8,128)S(1)}, f32[256,128]{1,0:T(8,128)S(1)}, u32[]{:S(2)}, u32[]{:S(2)}) collective-permute-start(f32[256,128]{1,0:T(8,128)S(1)} %get-tuple-element.84), channel_id=1, source_target_pairs={{0,2},{2,0},{4,6},{6,4},{8,10},{10,8},{12,14},{14,12},{16,18},{18,... | collective-permute-start | bytes 393224 | tf_op jit(solution)/shard_map/ppermute | solution.py:283
  30.7 5.5 %collective-permute-start.14 = (f32[256,128]{1,0:T(8,128)S(1)}, f32[256,128]{1,0:T(8,128)S(1)}, u32[]{:S(2)}, u32[]{:S(2)}) collective-permute-start(f32[256,128]{1,0:T(8,128)S(1)} %get-tuple-element.98), channel_id=1, source_target_pairs={{0,2},{2,0},{4,6},{6,4},{8,10},{10,8},{12,14},{14,12},{16,18},{18,... | collective-permute-start | bytes 393224 | tf_op jit(solution)/shard_map/ppermute | solution.py:283
  32.3 9.2 %collective-permute-start.18 = (f32[512,128]{1,0:T(8,128)S(1)}, f32[512,128]{1,0:T(8,128)S(1)}, u32[]{:S(2)}, u32[]{:S(2)}) collective-permute-start(f32[512,128]{1,0:T(8,128)S(1)} %expand.12), channel_id=1, source_target_pairs={{0,4},{2,6},{4,0},{6,2},{8,12},{10,14},{12,8},{14,10},{16,20},{18,... | collective-permute-start | bytes 786440 | tf_op jit(solution)/shard_map/ppermute | solution.py:283
  36.2 2.2 %collective-permute-start.13 = (f32[256,128]{1,0:T(8,128)S(1)}, f32[256,128]{1,0:T(8,128)S(1)}, u32[]{:S(2)}, u32[]{:S(2)}) collective-permute-start(f32[256,128]{1,0:T(8,128)S(1)} %get-tuple-element.96), channel_id=1, source_target_pairs={{0,2},{2,0},{4,6},{6,4},{8,10},{10,8},{12,14},{14,12},{16,18},{18,... | collective-permute-start | bytes 393224 | tf_op jit(solution)/shard_map/ppermute | solution.py:283
  36.3 9.2 %collective-permute-start.12 = (f32[512,128]{1,0:T(8,128)S(1)}, f32[512,128]{1,0:T(8,128)S(1)}, u32[]{:S(2)}, u32[]{:S(2)}) collective-permute-start(f32[512,128]{1,0:T(8,128)S(1)} %pad_maximum_fusion), channel_id=1, source_target_pairs={{0,8},{2,10},{4,12},{6,14},{8,0},{10,2},{12,4},{14,6},{16,24},{18,... | collective-permute-start | bytes 786440 | tf_op jit(solution)/shard_map/ppermute | solution.py:283
  37.9 2.1 %collective-permute-start.16 = (f32[256,128]{1,0:T(8,128)S(1)}, f32[256,128]{1,0:T(8,128)S(1)}, u32[]{:S(2)}, u32[]{:S(2)}) collective-permute-start(f32[256,128]{1,0:T(8,128)S(1)} %get-tuple-element.104), channel_id=1, source_target_pairs={{0,2},{2,0},{4,6},{6,4},{8,10},{10,8},{12,14},{14,12},{16,18},{18,... | collective-permute-start | bytes 393224 | tf_op jit(solution)/shard_map/ppermute | solution.py:283
  38.6 12.3 %collective-permute-start.17 = (f32[512,128]{1,0:T(8,128)S(1)}, f32[512,128]{1,0:T(8,128)S(1)}, u32[]{:S(2)}, u32[]{:S(2)}) collective-permute-start(f32[512,128]{1,0:T(8,128)S(1)} %expand.14), channel_id=1, source_target_pairs={{0,4},{2,6},{4,0},{6,2},{8,12},{10,14},{12,8},{14,10},{16,20},{18,... | collective-permute-start | bytes 786440 | tf_op jit(solution)/shard_map/ppermute | solution.py:283
  41.5 6.6 %collective-permute-start.19 = (f32[256,128]{1,0:T(8,128)S(1)}, f32[256,128]{1,0:T(8,128)S(1)}, u32[]{:S(2)}, u32[]{:S(2)}) collective-permute-start(f32[256,128]{1,0:T(8,128)S(1)} %slice_add_fusion), channel_id=1, source_target_pairs={{0,8},{2,10},{4,12},{6,14},{8,0},{10,2},{12,4},{14,6},{16,24},{18,... | collective-permute-start | bytes 393224 | tf_op jit(solution)/shard_map/ppermute | solution.py:283
  45.5 10.6 %collective-permute-start.15 = (f32[256,128]{1,0:T(8,128)S(1)}, f32[256,128]{1,0:T(8,128)S(1)}, u32[]{:S(2)}, u32[]{:S(2)}) collective-permute-start(f32[256,128]{1,0:T(8,128)S(1)} %pad_maximum_fusion.2), channel_id=1, source_target_pairs={{0,16},{2,18},{4,20},{6,22},{8,24},{10,26},{12,28},{14,30},{16,0},... | collective-permute-start | bytes 393224 | tf_op jit(solution)/shard_map/ppermute | solution.py:283
  48.2 8.7 %collective-permute-start.20 = (f32[128,128]{1,0:T(8,128)S(1)}, f32[128,128]{1,0:T(8,128)S(1)}, u32[]{:S(2)}, u32[]{:S(2)}) collective-permute-start(f32[128,128]{1,0:T(8,128)S(1)} %fusion.7), channel_id=1, source_target_pairs={{0,16},{2,18},{4,20},{6,22},{8,24},{10,26},{12,28},{14,30},{16,0},... | collective-permute-start | bytes 196616 | tf_op jit(solution)/shard_map/ppermute | solution.py:283
  50.9 7.1 %collective-permute-start.21 = (f32[256,128]{1,0:T(8,128)S(1)}, f32[256,128]{1,0:T(8,128)S(1)}, u32[]{:S(2)}, u32[]{:S(2)}) collective-permute-start(f32[256,128]{1,0:T(8,128)S(1)} %slice_add_fusion.1), channel_id=1, source_target_pairs={{0,8},{2,10},{4,12},{6,14},{8,0},{10,2},{12,4},{14,6},{16,24},{18,... | collective-permute-start | bytes 393224 | tf_op jit(solution)/shard_map/ppermute | solution.py:283
  58.1 5.9 %collective-permute-start.22 = (f32[128,128]{1,0:T(8,128)S(1)}, f32[128,128]{1,0:T(8,128)S(1)}, u32[]{:S(2)}, u32[]{:S(2)}) collective-permute-start(f32[128,128]{1,0:T(8,128)S(1)} %fusion), channel_id=1, source_target_pairs={{0,16},{2,18},{4,20},{6,22},{8,24},{10,26},{12,28},{14,30},{16,0},... | collective-permute-start | bytes 196616 | tf_op jit(solution)/shard_map/ppermute | solution.py:283

commit v2 on v1

--- a/solution.py
+++ b/solution.py
@@ -10,8 +10,7 @@
 F32 = jnp.float32
 BF16 = jnp.bfloat16
 CHUNK = 128
-FIRST = 52.5
-SECOND = 52
+ROW = 20_000_000_000
 
 
 def split(x):
@@ -228,7 +227,7 @@
                 pltpu.VMEM((box * rank, width), BF16),
                 pltpu.SemaphoreType.DMA((2 * pieces + 2 * levels + 1,)),
             ],
-            compiler_params=pltpu.CompilerParams(vmem_limit_bytes=int(limit * 2**20)),
+            compiler_params=pltpu.CompilerParams(vmem_limit_bytes=limit * 2**20),
             cost_estimate=cost,
             name="column_side",
         )(right_sides, proj, col, mid)
@@ -264,7 +263,7 @@
             out_shape=[quarter] * 4,
             scratch_shapes=[pltpu.VMEM((box * rank, CHUNK), t) for t in (BF16, BF16, F32)],
             compiler_params=params,
-            cost_estimate=pl.CostEstimate(flops=20_000_000_000, bytes_accessed=100_000, transcendentals=0),
+            cost_estimate=pl.CostEstimate(flops=ROW, bytes_accessed=100_000, transcendentals=0),
             name="row_side",
         )(*parts, wide)
 
@@ -292,12 +291,12 @@
         left = terms[-1].shape[0]
         return total(terms, left // 2, left)
 
-    parts = column_side(0, 2, mid, FIRST)
+    parts = column_side(0, 1, mid, 53)
     received = {0: exchange(parts[0])}
-    parts += column_side(2, chunks - 2, tie(mid, parts[0][-1]), SECOND)
+    parts += column_side(1, chunks - 1, tie(mid, parts[0][-1]), 52)
     received[1] = exchange(parts[1])
     wide = row_weights()
-    last_wide = expand_weights(swap(tie(expand, parts[-1][0]), "tile", n_tile, 1))
+    last_wide = expand_weights(swap(tie(expand, wide), "tile", n_tile, 1))
 
     terms, sends, lows = [], {}, []
     last = chunks - 1
@@ -320,32 +319,29 @@
 
     early = list(range(last - 1))
     for c in range(chunks):
-        after = sends[c - 1, 1] if c else parts[-1][0]
-        own_low, own_high, low, high = row_side([tie(x, after) for x in received[c]], wide)
+        after = [sends[c - 1, 1]] if c else [parts[-1][0]]
+        if c == last:
+            after.append(forward(early, 2, sends[c - 1, 1]))
+        own_low, own_high, low, high = row_side([tie(x, *after) for x in received[c]], wide)
         lows.append((own_low, swap(low, "tile", n_tile, 1)))
         done = []
         if c >= 1:
             done.append(low_half(c - 1, own_high))
-        if c == last:
-            done.append(forward(early, 2, own_high))
         got = swap(high, "tile", n_tile, 1)
         if done:
             got = tie(got, *done)
         sends[c, 1] = expanded(1, own_high, got, last_wide)
         terms.append([None, swap(sends[c, 1], "tile", n_tile, 2)])
         if c + 2 < chunks:
-            received[c + 2] = exchange(parts[c + 2], sends[c, 1])
+            received[c + 2] = exchange(parts[c + 2], own_high)
     low_half(last, sends[last, 1])
-    done = [forward([last - 1], 2, sends[last, 1])]
-    if bits > 3:
-        done += [forward(group, 3, sends[last, 1]) for group in (early, [last - 1])]
-    forward([last], 2, *done)
-    for b in range(3, bits):
+    done = sends[last, 1]
+    for group, b in ((early, 3), ([last - 1], 2), ([last], 2), ([last - 1], 3), ([last], 3)):
+        if b < bits:
+            done = forward(group, b, done)
+    for b in range(4, bits):
         for group in (early, [last - 1], [last]):
-            if (group[-1], b) not in sends:
-                forward(group, b, sends[last, 2])
-    for c in range(last):
-        terms[c][-1] = tie(terms[c][-1], sends[last, 2])
+            done = forward(group, b, done)
     return jnp.concatenate([total(t, 0, out_rows) for t in terms], axis=1)
 
 

time: 64.9 us -> 60.4 us (0.931)
  starting transfers between devices: 26.5 us -> 21.5 us
  local copies, waits for them, and re-layouts: 0.04 us -> 0.81 us
    ppermute x23, starting transfers between devices: 26.5 us -> 21.5 us  [swap(): return lax.ppermute(x, axis, [(i, i ^ mask) for i in range(size)])]
    unnamed x6 -> x4, local copies, waits for them, and re-layouts: 0.02 us -> 0.79 us
  transfers between devices with their start and end apart: 23 -> 23, of which waited for: 12 -> 11; matrix products, arithmetic and copies ran while one was open for 0% -> 0% of each run, Pallas kernels for 18% -> 21%
where the time goes in v2:
time: 60.4 us; the launch traced here: 60.3 us
  starting transfers between devices  21.5 us (36%)
  waiting for transfers between devices  20.2 us (33%)
  Pallas kernels  16.6 us (27%)
  other arithmetic  0.93 us (2%)
  local copies, waits for them, and re-layouts  0.81 us (1%)
    ppermute x23, starting transfers between devices, swap(): return lax.ppermute(x, axis, [(i, i ^ mask) for i in range(size)])  21.5 us
    ppermute x23, waiting for transfers between devices, swap(): return lax.ppermute(x, axis, [(i, i ^ mask) for i in range(size)])  20.2 us
    pallas_call x2, Pallas kernels, column_side(): pl.pallas_call(functools.partial(column_kernel, n_seg, pieces, start * CH...  9.49 us
    pallas_call x4, Pallas kernels, row_side(): pl.pallas_call(functools.partial(row_kernel, n_seg, n_tile, leaf), in_spe...  4.71 us
    pallas_call x8, Pallas kernels, expanded(): pl.pallas_call(functools.partial(expand_kernel, part), in_specs=[in_vmem]...  1.89 us
  transfers between devices with their start and end apart: 23, of which 11 were waited for; matrix products, arithmetic and copies ran while one was open for 0% of the time, Pallas kernels for 21%

profile of v2, /device:TPU:0, one launch (start us, length us, event | category | flops | bytes accessed | tf_op | source)
XLA Modules:
  0.0 60.3 jit_solution(12145721609243673916)
XLA Ops:
  0.0 3.7 %column_side.2 = (f32[512,128]{1,0:T(8,128)S(1)}, f32[512,128]{1,0:T(8,128)S(1)}) custom-call(f32[2048,512]{1,0:T(8,128)} %x_hbm.3, f32[16,64,128]{2,1,0:T(8,128)} %bitcast.12, f32[4,8,128,128]{3,2,1,0:T(8,128)} %bitcast.10, f32[16,64,64]{2,1,0:T(8,128)} %bitcast.14), custom_call_target="tpu_custom_call" | custom-call | flops 1000000 | bytes 100000 | tf_op jit(solution)/shard_map/column_side/pallas_call | solution.py:216
  3.7 0.0 copy-start
  3.7 3.0 %collective-permute-start = (f32[512,128]{1,0:T(8,128)S(1)}, f32[512,128]{1,0:T(8,128)S(1)}, u32[]{:S(2)}, u32[]{:S(2)}) collective-permute-start(f32[512,128]{1,0:T(8,128)S(1)} %get-tuple-element.57), channel_id=1, source_target_pairs={{0,1},{1,0},{2,3},{3,2},{4,5},{5,4},{6,7},{7,6},{8,9},{9,8},{10,11... | collective-permute-start | bytes 786440 | tf_op jit(solution)/shard_map/ppermute | solution.py:282
  6.7 5.8 %column_side.3 = (f32[512,128]{1,0:T(8,128)S(1)}, f32[512,128]{1,0:T(8,128)S(1)}, f32[512,128]{1,0:T(8,128)S(1)}, f32[512,128]{1,0:T(8,128)S(1)}, f32[512,128]{1,0:T(8,128)S(1)}, /*index=5*/f32[512,128]{1,0:T(8,128)S(1)}) custom-call(f32[2048,512]{1,0:T(8,128)} %x_hbm.3, f32[16,64,128]{2,1,0:T(8,128)} %bitcast.13, f32[4,8,128,128]{3,2,1,0:T(8,128)} %bitcast.11, ...), custom_call_target="tpu_custom_call" | custom-call | flops 1000000 | bytes 100000 | tf_op jit(solution)/shard_map/column_side/pallas_call | solution.py:216
  12.5 0.2 collective-permute-start.4
  12.7 0.3 row_weights.1.refs_2_
  13.0 0.8 %copy-done.1 = f32[1,16,128,64]{2,3,1,0:T(8,128)S(1)} copy-done((f32[1,16,128,64]{2,3,1,0:T(8,128)S(1)}, f32[1,16,128,64]{2,3,1,0:T(8,128)}, u32[]{:S(2)}) %copy-start.1) | copy-done | bytes 524312
  13.8 0.0 collective-permute-start.3
  13.8 0.0 collective-permute-done.refs_1_
  13.8 1.2 %row_side.4 = (f32[256,128]{1,0:T(8,128)S(1)}, f32[256,128]{1,0:T(8,128)S(1)}, f32[256,128]{1,0:T(8,128)S(1)}, f32[256,128]{1,0:T(8,128)S(1)}) custom-call(f32[512,128]{1,0:T(8,128)S(1)} %get-tuple-element.60.refs_0_, f32[512,128]{1,0:T(8,128)S(1)} %collective-permute-done.refs_1_, bf16[4,8,128,256]{3,2,1,0:T(8,128)(2,1)S(1)} %row_weights.1.refs_2_), custom_call_target="tpu_custom_call" | custom-call | flops 20000000000 | bytes 100000 | tf_op jit(solution)/shard_map/row_side/pallas_call | solution.py:259
  15.0 0.6 collective-permute-start.2
  15.5 0.1 collective-permute-start.1
  15.6 1.9 %collective-permute-start.7 = (f32[512,128]{1,0:T(8,128)S(1)}, f32[512,128]{1,0:T(8,128)S(1)}, u32[]{:S(2)}, u32[]{:S(2)}) collective-permute-start(f32[512,128]{1,0:T(8,128)S(1)} %get-tuple-element.78), channel_id=1, source_target_pairs={{0,1},{1,0},{2,3},{3,2},{4,5},{5,4},{6,7},{7,6},{8,9},{9,8},{10,11... | collective-permute-start | bytes 786440 | tf_op jit(solution)/shard_map/ppermute | solution.py:282
  17.5 0.0 collective-permute-done.3.other_ref
  17.5 0.2 expand_weights.1.last_ref
  17.7 0.0 collective-permute-done.2.other_ref
  17.7 0.2 expand.8
  18.0 1.6 %collective-permute-start.5 = (f32[512,128]{1,0:T(8,128)S(1)}, f32[512,128]{1,0:T(8,128)S(1)}, u32[]{:S(2)}, u32[]{:S(2)}) collective-permute-start(f32[512,128]{1,0:T(8,128)S(1)} %expand.8), channel_id=1, source_target_pairs={{0,4},{2,6},{4,0},{6,2},{8,12},{10,14},{12,8},{14,10},{16,20},{18,... | collective-permute-start | bytes 786440 | tf_op jit(solution)/shard_map/ppermute | solution.py:282
  19.6 2.3 %collective-permute-done.4.refs_1_ = f32[512,128]{1,0:T(8,128)S(1)} collective-permute-done((f32[512,128]{1,0:T(8,128)S(1)}, f32[512,128]{1,0:T(8,128)S(1)}, u32[]{:S(2)}, u32[]{:S(2)}) %collective-permute-start.4) | collective-permute-done | bytes 262176 | tf_op jit(solution)/shard_map/ppermute | solution.py:282
  21.8 1.2 %row_side.5 = (f32[256,128]{1,0:T(8,128)S(1)}, f32[256,128]{1,0:T(8,128)S(1)}, f32[256,128]{1,0:T(8,128)S(1)}, f32[256,128]{1,0:T(8,128)S(1)}) custom-call(f32[512,128]{1,0:T(8,128)S(1)} %get-tuple-element.68.refs_0_, f32[512,128]{1,0:T(8,128)S(1)} %collective-permute-done.4.refs_1_, bf16[4,8,128,256]{3,2,1,0:T(8,128)(2,1)S(1)} %row_weights.1.refs_2_), custom_call_target="tpu_custom_call" | custom-call | flops 20000000000 | bytes 100000 | tf_op jit(solution)/shard_map/row_side/pallas_call | solution.py:259
  23.0 0.0 collective-permute-done.1.other_ref
  23.0 0.1 collective-permute-start.6
  23.1 0.5 collective-permute-start.9
  23.6 0.0 collective-permute-start.12
  23.6 0.2 expand.9
  23.8 0.6 collective-permute-done.6.other_ref
  24.4 0.2 expand.10
  24.7 1.3 %collective-permute-start.10 = (f32[512,128]{1,0:T(8,128)S(1)}, f32[512,128]{1,0:T(8,128)S(1)}, u32[]{:S(2)}, u32[]{:S(2)}) collective-permute-start(f32[512,128]{1,0:T(8,128)S(1)} %expand.10), channel_id=1, source_target_pairs={{0,4},{2,6},{4,0},{6,2},{8,12},{10,14},{12,8},{14,10},{16,20},{18,... | collective-permute-start | bytes 786440 | tf_op jit(solution)/shard_map/ppermute | solution.py:282
  26.0 0.0 collective-permute-done.7.refs_1_
  26.0 1.2 %row_side.6 = (f32[256,128]{1,0:T(8,128)S(1)}, f32[256,128]{1,0:T(8,128)S(1)}, f32[256,128]{1,0:T(8,128)S(1)}, f32[256,128]{1,0:T(8,128)S(1)}) custom-call(f32[512,128]{1,0:T(8,128)S(1)} %get-tuple-element.76.refs_0_, f32[512,128]{1,0:T(8,128)S(1)} %collective-permute-done.7.refs_1_, bf16[4,8,128,256]{3,2,1,0:T(8,128)(2,1)S(1)} %row_weights.1.refs_2_), custom_call_target="tpu_custom_call" | custom-call | flops 20000000000 | bytes 100000 | tf_op jit(solution)/shard_map/row_side/pallas_call | solution.py:259
  27.2 0.1 collective-permute-start.8
  27.3 0.0 collective-permute-done.9.other_ref
  27.3 0.5 collective-permute-start.14
  27.8 0.2 expand.11
  28.0 0.6 collective-permute-done.8.other_ref
  28.6 0.2 expand.12
  28.9 1.5 %collective-permute-start.16 = (f32[512,128]{1,0:T(8,128)S(1)}, f32[512,128]{1,0:T(8,128)S(1)}, u32[]{:S(2)}, u32[]{:S(2)}) collective-permute-start(f32[512,128]{1,0:T(8,128)S(1)} %expand.12), channel_id=1, source_target_pairs={{0,4},{2,6},{4,0},{6,2},{8,12},{10,14},{12,8},{14,10},{16,20},{18,... | collective-permute-start | bytes 786440 | tf_op jit(solution)/shard_map/ppermute | solution.py:282
  30.4 0.0 collective-permute-done.5
  30.4 3.5 %collective-permute-done.10 = f32[512,128]{1,0:T(8,128)S(1)} collective-permute-done((f32[512,128]{1,0:T(8,128)S(1)}, f32[512,128]{1,0:T(8,128)S(1)}, u32[]{:S(2)}, u32[]{:S(2)}) %collective-permute-start.10) | collective-permute-done | bytes 262176 | tf_op jit(solution)/shard_map/ppermute | solution.py:282
  33.9 1.4 %collective-permute-start.11 = (f32[512,128]{1,0:T(8,128)S(1)}, f32[512,128]{1,0:T(8,128)S(1)}, u32[]{:S(2)}, u32[]{:S(2)}) collective-permute-start(f32[512,128]{1,0:T(8,128)S(1)} %pad_maximum_fusion), channel_id=1, source_target_pairs={{0,8},{2,10},{4,12},{6,14},{8,0},{10,2},{12,4},{14,6},{16,24},{18,... | collective-permute-start | bytes 786440 | tf_op jit(solution)/shard_map/ppermute | solution.py:282
  35.3 0.0 collective-permute-done.12.refs_1_
  35.3 1.2 %row_side.7 = (f32[256,128]{1,0:T(8,128)S(1)}, f32[256,128]{1,0:T(8,128)S(1)}, f32[256,128]{1,0:T(8,128)S(1)}, f32[256,128]{1,0:T(8,128)S(1)}) custom-call(f32[512,128]{1,0:T(8,128)S(1)} %get-tuple-element.88.refs_0_, f32[512,128]{1,0:T(8,128)S(1)} %collective-permute-done.12.refs_1_, bf16[4,8,128,256]{3,2,1,0:T(8,128)(2,1)S(1)} %row_weights.1.refs_2_), custom_call_target="tpu_custom_call" | custom-call | flops 20000000000 | bytes 100000 | tf_op jit(solution)/shard_map/row_side/pallas_call | solution.py:259
  36.5 0.0 collective-permute-done.14.other_ref
  36.5 0.1 collective-permute-start.13
  36.6 0.5 collective-permute-start.18
  37.1 0.2 expand.13
  37.3 0.6 collective-permute-done.13.other_ref
  37.9 0.2 expand.14
  38.2 1.6 %collective-permute-start.19 = (f32[512,128]{1,0:T(8,128)S(1)}, f32[512,128]{1,0:T(8,128)S(1)}, u32[]{:S(2)}, u32[]{:S(2)}) collective-permute-start(f32[512,128]{1,0:T(8,128)S(1)} %expand.14), channel_id=1, source_target_pairs={{0,4},{2,6},{4,0},{6,2},{8,12},{10,14},{12,8},{14,10},{16,20},{18,... | collective-permute-start | bytes 786440 | tf_op jit(solution)/shard_map/ppermute | solution.py:282
  39.8 0.0 collective-permute-done.18.other_ref
  39.8 0.2 expand.15
  40.0 0.7 %collective-permute-done.11 = f32[512,128]{1,0:T(8,128)S(1)} collective-permute-done((f32[512,128]{1,0:T(8,128)S(1)}, f32[512,128]{1,0:T(8,128)S(1)}, u32[]{:S(2)}, u32[]{:S(2)}) %collective-permute-start.11) | collective-permute-done | bytes 262176 | tf_op jit(solution)/shard_map/ppermute | solution.py:282
  40.8 2.4 %collective-permute-start.15 = (f32[256,128]{1,0:T(8,128)S(1)}, f32[256,128]{1,0:T(8,128)S(1)}, u32[]{:S(2)}, u32[]{:S(2)}) collective-permute-start(f32[256,128]{1,0:T(8,128)S(1)} %pad_maximum_fusion.2), channel_id=1, source_target_pairs={{0,16},{2,18},{4,20},{6,22},{8,24},{10,26},{12,28},{14,30},{16,0},... | collective-permute-start | bytes 393224 | tf_op jit(solution)/shard_map/ppermute | solution.py:282
  43.2 0.0 collective-permute-done.16
  43.2 1.7 %collective-permute-start.17 = (f32[256,128]{1,0:T(8,128)S(1)}, f32[256,128]{1,0:T(8,128)S(1)}, u32[]{:S(2)}, u32[]{:S(2)}) collective-permute-start(f32[256,128]{1,0:T(8,128)S(1)} %slice_add_fusion.1), channel_id=1, source_target_pairs={{0,8},{2,10},{4,12},{6,14},{8,0},{10,2},{12,4},{14,6},{16,24},{18,... | collective-permute-start | bytes 393224 | tf_op jit(solution)/shard_map/ppermute | solution.py:282
  44.9 1.7 %collective-permute-done.19 = f32[512,128]{1,0:T(8,128)S(1)} collective-permute-done((f32[512,128]{1,0:T(8,128)S(1)}, f32[512,128]{1,0:T(8,128)S(1)}, u32[]{:S(2)}, u32[]{:S(2)}) %collective-permute-start.19) | collective-permute-done | bytes 262176 | tf_op jit(solution)/shard_map/ppermute | solution.py:282
  46.6 0.8 %collective-permute-start.21 = (f32[256,128]{1,0:T(8,128)S(1)}, f32[256,128]{1,0:T(8,128)S(1)}, u32[]{:S(2)}, u32[]{:S(2)}) collective-permute-start(f32[256,128]{1,0:T(8,128)S(1)} %slice_add_fusion), channel_id=1, source_target_pairs={{0,8},{2,10},{4,12},{6,14},{8,0},{10,2},{12,4},{14,6},{16,24},{18,... | collective-permute-start | bytes 393224 | tf_op jit(solution)/shard_map/ppermute | solution.py:282
  47.4 3.7 %collective-permute-done.17 = f32[256,128]{1,0:T(8,128)S(1)} collective-permute-done((f32[256,128]{1,0:T(8,128)S(1)}, f32[256,128]{1,0:T(8,128)S(1)}, u32[]{:S(2)}, u32[]{:S(2)}) %collective-permute-start.17) | collective-permute-done | bytes 131104 | tf_op jit(solution)/shard_map/ppermute | solution.py:282
  51.1 0.1 collective-permute-start.20
  51.2 2.1 %collective-permute-done.21 = f32[256,128]{1,0:T(8,128)S(1)} collective-permute-done((f32[256,128]{1,0:T(8,128)S(1)}, f32[256,128]{1,0:T(8,128)S(1)}, u32[]{:S(2)}, u32[]{:S(2)}) %collective-permute-start.21) | collective-permute-done | bytes 131104 | tf_op jit(solution)/shard_map/ppermute | solution.py:282
  53.3 1.8 %collective-permute-start.22 = (f32[128,128]{1,0:T(8,128)S(1)}, f32[128,128]{1,0:T(8,128)S(1)}, u32[]{:S(2)}, u32[]{:S(2)}) collective-permute-start(f32[128,128]{1,0:T(8,128)S(1)} %fusion), channel_id=1, source_target_pairs={{0,16},{2,18},{4,20},{6,22},{8,24},{10,26},{12,28},{14,30},{16,0},... | collective-permute-start | bytes 196616 | tf_op jit(solution)/shard_map/ppermute | solution.py:282
  55.0 2.8 %collective-permute-done.20 = f32[128,128]{1,0:T(8,128)S(1)} collective-permute-done((f32[128,128]{1,0:T(8,128)S(1)}, f32[128,128]{1,0:T(8,128)S(1)}, u32[]{:S(2)}, u32[]{:S(2)}) %collective-permute-start.20) | collective-permute-done | bytes 65568 | tf_op jit(solution)/shard_map/ppermute | solution.py:282
  57.9 1.6 %collective-permute-done.22 = f32[128,128]{1,0:T(8,128)S(1)} collective-permute-done((f32[128,128]{1,0:T(8,128)S(1)}, f32[128,128]{1,0:T(8,128)S(1)}, u32[]{:S(2)}, u32[]{:S(2)}) %collective-permute-start.22) | collective-permute-done | bytes 65568 | tf_op jit(solution)/shard_map/ppermute | solution.py:282
  59.5 0.7 %pad_maximum_fusion.1 = f32[128,512]{1,0:T(8,128)} fusion(f32[128,128]{1,0:T(8,128)S(1)} %fusion.2, f32[128,128]{1,0:T(8,128)S(1)} %fusion.5, f32[128,128]{1,0:T(8,128)S(1)} %get-tuple-element.110, f32[128,128]{1,0:T(8,128)S(1)} %get-tuple-element.109), kind=kLoop, calls=%fused_computation.1 | loop fusion | flops 196608 | bytes 524288 | tf_op jit(solution)/shard_map/concatenate | solution.py:345
  (16 shorter events, 0.2 us)
Async XLA Ops:
  3.7 9.0 %copy-start = (f32[1,4,8,128,128]{4,3,2,1,0:T(8,128)S(1)}, f32[1,4,8,128,128]{4,3,2,1,0:T(8,128)}, u32[]{:S(2)}) copy-start(f32[1,4,8,128,128]{4,3,2,1,0:T(8,128)} %param.10) | copy-start | bytes 6291460
  3.7 10.1 %collective-permute-start = (f32[512,128]{1,0:T(8,128)S(1)}, f32[512,128]{1,0:T(8,128)S(1)}, u32[]{:S(2)}, u32[]{:S(2)}) collective-permute-start(f32[512,128]{1,0:T(8,128)S(1)} %get-tuple-element.57), channel_id=1, source_target_pairs={{0,1},{1,0},{2,3},{3,2},{4,5},{5,4},{6,7},{7,6},{8,9},{9,8},{10,11... | collective-permute-start | bytes 786440 | tf_op jit(solution)/shard_map/ppermute | solution.py:282
  12.5 9.3 %collective-permute-start.4 = (f32[512,128]{1,0:T(8,128)S(1)}, f32[512,128]{1,0:T(8,128)S(1)}, u32[]{:S(2)}, u32[]{:S(2)}) collective-permute-start(f32[512,128]{1,0:T(8,128)S(1)} %get-tuple-element.69), channel_id=1, source_target_pairs={{0,1},{1,0},{2,3},{3,2},{4,5},{5,4},{6,7},{7,6},{8,9},{9,8},{10,11... | collective-permute-start | bytes 786440 | tf_op jit(solution)/shard_map/ppermute | solution.py:282
  12.7 1.0 %copy-start.1 = (f32[1,16,128,64]{2,3,1,0:T(8,128)S(1)}, f32[1,16,128,64]{2,3,1,0:T(8,128)}, u32[]{:S(2)}) copy-start(f32[1,16,128,64]{2,3,1,0:T(8,128)} %param.11) | copy-start | bytes 1572868
  13.8 3.7 %collective-permute-start.3 = (f32[16,64,128]{2,1,0:T(8,128)S(1)}, f32[16,64,128]{2,1,0:T(8,128)S(1)}, u32[]{:S(2)}, u32[]{:S(2)}) collective-permute-start(f32[16,64,128]{2,1,0:T(8,128)S(1)} %bitcast.8), channel_id=1, source_target_pairs={{0,2},{2,0},{4,6},{6,4},{8,10},{10,8},{12,14},{14,12},{16,18},{18,... | collective-permute-start | bytes 1572872 | tf_op jit(solution)/shard_map/ppermute | solution.py:282
  15.0 2.8 %collective-permute-start.2 = (f32[256,128]{1,0:T(8,128)S(1)}, f32[256,128]{1,0:T(8,128)S(1)}, u32[]{:S(2)}, u32[]{:S(2)}) collective-permute-start(f32[256,128]{1,0:T(8,128)S(1)} %get-tuple-element.66), channel_id=1, source_target_pairs={{0,2},{2,0},{4,6},{6,4},{8,10},{10,8},{12,14},{14,12},{16,18},{18,... | collective-permute-start | bytes 393224 | tf_op jit(solution)/shard_map/ppermute | solution.py:282
  15.5 7.5 %collective-permute-start.1 = (f32[256,128]{1,0:T(8,128)S(1)}, f32[256,128]{1,0:T(8,128)S(1)}, u32[]{:S(2)}, u32[]{:S(2)}) collective-permute-start(f32[256,128]{1,0:T(8,128)S(1)} %get-tuple-element.63), channel_id=1, source_target_pairs={{0,2},{2,0},{4,6},{6,4},{8,10},{10,8},{12,14},{14,12},{16,18},{18,... | collective-permute-start | bytes 393224 | tf_op jit(solution)/shard_map/ppermute | solution.py:282
  15.6 10.4 %collective-permute-start.7 = (f32[512,128]{1,0:T(8,128)S(1)}, f32[512,128]{1,0:T(8,128)S(1)}, u32[]{:S(2)}, u32[]{:S(2)}) collective-permute-start(f32[512,128]{1,0:T(8,128)S(1)} %get-tuple-element.78), channel_id=1, source_target_pairs={{0,1},{1,0},{2,3},{3,2},{4,5},{5,4},{6,7},{7,6},{8,9},{9,8},{10,11... | collective-permute-start | bytes 786440 | tf_op jit(solution)/shard_map/ppermute | solution.py:282
  18.0 12.4 %collective-permute-start.5 = (f32[512,128]{1,0:T(8,128)S(1)}, f32[512,128]{1,0:T(8,128)S(1)}, u32[]{:S(2)}, u32[]{:S(2)}) collective-permute-start(f32[512,128]{1,0:T(8,128)S(1)} %expand.8), channel_id=1, source_target_pairs={{0,4},{2,6},{4,0},{6,2},{8,12},{10,14},{12,8},{14,10},{16,20},{18,... | collective-permute-start | bytes 786440 | tf_op jit(solution)/shard_map/ppermute | solution.py:282
  23.0 1.4 %collective-permute-start.6 = (f32[256,128]{1,0:T(8,128)S(1)}, f32[256,128]{1,0:T(8,128)S(1)}, u32[]{:S(2)}, u32[]{:S(2)}) collective-permute-start(f32[256,128]{1,0:T(8,128)S(1)} %get-tuple-element.74), channel_id=1, source_target_pairs={{0,2},{2,0},{4,6},{6,4},{8,10},{10,8},{12,14},{14,12},{16,18},{18,... | collective-permute-start | bytes 393224 | tf_op jit(solution)/shard_map/ppermute | solution.py:282
  23.1 4.2 %collective-permute-start.9 = (f32[256,128]{1,0:T(8,128)S(1)}, f32[256,128]{1,0:T(8,128)S(1)}, u32[]{:S(2)}, u32[]{:S(2)}) collective-permute-start(f32[256,128]{1,0:T(8,128)S(1)} %get-tuple-element.83), channel_id=1, source_target_pairs={{0,2},{2,0},{4,6},{6,4},{8,10},{10,8},{12,14},{14,12},{16,18},{18,... | collective-permute-start | bytes 393224 | tf_op jit(solution)/shard_map/ppermute | solution.py:282
  23.6 11.7 %collective-permute-start.12 = (f32[512,128]{1,0:T(8,128)S(1)}, f32[512,128]{1,0:T(8,128)S(1)}, u32[]{:S(2)}, u32[]{:S(2)}) collective-permute-start(f32[512,128]{1,0:T(8,128)S(1)} %get-tuple-element.90), channel_id=1, source_target_pairs={{0,1},{1,0},{2,3},{3,2},{4,5},{5,4},{6,7},{7,6},{8,9},{9,8},{10,11... | collective-permute-start | bytes 786440 | tf_op jit(solution)/shard_map/ppermute | solution.py:282
  24.7 9.2 %collective-permute-start.10 = (f32[512,128]{1,0:T(8,128)S(1)}, f32[512,128]{1,0:T(8,128)S(1)}, u32[]{:S(2)}, u32[]{:S(2)}) collective-permute-start(f32[512,128]{1,0:T(8,128)S(1)} %expand.10), channel_id=1, source_target_pairs={{0,4},{2,6},{4,0},{6,2},{8,12},{10,14},{12,8},{14,10},{16,20},{18,... | collective-permute-start | bytes 786440 | tf_op jit(solution)/shard_map/ppermute | solution.py:282
  27.2 1.4 %collective-permute-start.8 = (f32[256,128]{1,0:T(8,128)S(1)}, f32[256,128]{1,0:T(8,128)S(1)}, u32[]{:S(2)}, u32[]{:S(2)}) collective-permute-start(f32[256,128]{1,0:T(8,128)S(1)} %get-tuple-element.81), channel_id=1, source_target_pairs={{0,2},{2,0},{4,6},{6,4},{8,10},{10,8},{12,14},{14,12},{16,18},{18,... | collective-permute-start | bytes 393224 | tf_op jit(solution)/shard_map/ppermute | solution.py:282
  27.3 9.2 %collective-permute-start.14 = (f32[256,128]{1,0:T(8,128)S(1)}, f32[256,128]{1,0:T(8,128)S(1)}, u32[]{:S(2)}, u32[]{:S(2)}) collective-permute-start(f32[256,128]{1,0:T(8,128)S(1)} %get-tuple-element.95), channel_id=1, source_target_pairs={{0,2},{2,0},{4,6},{6,4},{8,10},{10,8},{12,14},{14,12},{16,18},{18,... | collective-permute-start | bytes 393224 | tf_op jit(solution)/shard_map/ppermute | solution.py:282
  28.9 14.4 %collective-permute-start.16 = (f32[512,128]{1,0:T(8,128)S(1)}, f32[512,128]{1,0:T(8,128)S(1)}, u32[]{:S(2)}, u32[]{:S(2)}) collective-permute-start(f32[512,128]{1,0:T(8,128)S(1)} %expand.12), channel_id=1, source_target_pairs={{0,4},{2,6},{4,0},{6,2},{8,12},{10,14},{12,8},{14,10},{16,20},{18,... | collective-permute-start | bytes 786440 | tf_op jit(solution)/shard_map/ppermute | solution.py:282
  33.9 6.8 %collective-permute-start.11 = (f32[512,128]{1,0:T(8,128)S(1)}, f32[512,128]{1,0:T(8,128)S(1)}, u32[]{:S(2)}, u32[]{:S(2)}) collective-permute-start(f32[512,128]{1,0:T(8,128)S(1)} %pad_maximum_fusion), channel_id=1, source_target_pairs={{0,8},{2,10},{4,12},{6,14},{8,0},{10,2},{12,4},{14,6},{16,24},{18,... | collective-permute-start | bytes 786440 | tf_op jit(solution)/shard_map/ppermute | solution.py:282
  36.5 1.4 %collective-permute-start.13 = (f32[256,128]{1,0:T(8,128)S(1)}, f32[256,128]{1,0:T(8,128)S(1)}, u32[]{:S(2)}, u32[]{:S(2)}) collective-permute-start(f32[256,128]{1,0:T(8,128)S(1)} %get-tuple-element.93), channel_id=1, source_target_pairs={{0,2},{2,0},{4,6},{6,4},{8,10},{10,8},{12,14},{14,12},{16,18},{18,... | collective-permute-start | bytes 393224 | tf_op jit(solution)/shard_map/ppermute | solution.py:282
  36.6 3.2 %collective-permute-start.18 = (f32[256,128]{1,0:T(8,128)S(1)}, f32[256,128]{1,0:T(8,128)S(1)}, u32[]{:S(2)}, u32[]{:S(2)}) collective-permute-start(f32[256,128]{1,0:T(8,128)S(1)} %get-tuple-element.102), channel_id=1, source_target_pairs={{0,2},{2,0},{4,6},{6,4},{8,10},{10,8},{12,14},{14,12},{16,18},{18,... | collective-permute-start | bytes 393224 | tf_op jit(solution)/shard_map/ppermute | solution.py:282
  38.2 8.4 %collective-permute-start.19 = (f32[512,128]{1,0:T(8,128)S(1)}, f32[512,128]{1,0:T(8,128)S(1)}, u32[]{:S(2)}, u32[]{:S(2)}) collective-permute-start(f32[512,128]{1,0:T(8,128)S(1)} %expand.14), channel_id=1, source_target_pairs={{0,4},{2,6},{4,0},{6,2},{8,12},{10,14},{12,8},{14,10},{16,20},{18,... | collective-permute-start | bytes 786440 | tf_op jit(solution)/shard_map/ppermute | solution.py:282
  40.8 10.3 %collective-permute-start.15 = (f32[256,128]{1,0:T(8,128)S(1)}, f32[256,128]{1,0:T(8,128)S(1)}, u32[]{:S(2)}, u32[]{:S(2)}) collective-permute-start(f32[256,128]{1,0:T(8,128)S(1)} %pad_maximum_fusion.2), channel_id=1, source_target_pairs={{0,16},{2,18},{4,20},{6,22},{8,24},{10,26},{12,28},{14,30},{16,0},... | collective-permute-start | bytes 393224 | tf_op jit(solution)/shard_map/ppermute | solution.py:282
  43.2 7.8 %collective-permute-start.17 = (f32[256,128]{1,0:T(8,128)S(1)}, f32[256,128]{1,0:T(8,128)S(1)}, u32[]{:S(2)}, u32[]{:S(2)}) collective-permute-start(f32[256,128]{1,0:T(8,128)S(1)} %slice_add_fusion.1), channel_id=1, source_target_pairs={{0,8},{2,10},{4,12},{6,14},{8,0},{10,2},{12,4},{14,6},{16,24},{18,... | collective-permute-start | bytes 393224 | tf_op jit(solution)/shard_map/ppermute | solution.py:282
  46.6 6.6 %collective-permute-start.21 = (f32[256,128]{1,0:T(8,128)S(1)}, f32[256,128]{1,0:T(8,128)S(1)}, u32[]{:S(2)}, u32[]{:S(2)}) collective-permute-start(f32[256,128]{1,0:T(8,128)S(1)} %slice_add_fusion), channel_id=1, source_target_pairs={{0,8},{2,10},{4,12},{6,14},{8,0},{10,2},{12,4},{14,6},{16,24},{18,... | collective-permute-start | bytes 393224 | tf_op jit(solution)/shard_map/ppermute | solution.py:282
  51.1 6.8 %collective-permute-start.20 = (f32[128,128]{1,0:T(8,128)S(1)}, f32[128,128]{1,0:T(8,128)S(1)}, u32[]{:S(2)}, u32[]{:S(2)}) collective-permute-start(f32[128,128]{1,0:T(8,128)S(1)} %fusion.3), channel_id=1, source_target_pairs={{0,16},{2,18},{4,20},{6,22},{8,24},{10,26},{12,28},{14,30},{16,0},... | collective-permute-start | bytes 196616 | tf_op jit(solution)/shard_map/ppermute | solution.py:282
  53.3 6.3 %collective-permute-start.22 = (f32[128,128]{1,0:T(8,128)S(1)}, f32[128,128]{1,0:T(8,128)S(1)}, u32[]{:S(2)}, u32[]{:S(2)}) collective-permute-start(f32[128,128]{1,0:T(8,128)S(1)} %fusion), channel_id=1, source_target_pairs={{0,16},{2,18},{4,20},{6,22},{8,24},{10,26},{12,28},{14,30},{16,0},... | collective-permute-start | bytes 196616 | tf_op jit(solution)/shard_map/ppermute | solution.py:282

commit v3 on v2

--- a/solution.py
+++ b/solution.py
@@ -11,6 +11,7 @@
 BF16 = jnp.bfloat16
 CHUNK = 128
 ROW = 20_000_000_000
+LOW = 1
 
 
 def split(x):
@@ -128,25 +129,35 @@
     return relative, out_rows, min(out_rows, leaf), max(1, out_rows // leaf)
 
 
-def weights_kernel(row_ref, wide_ref):
+def weights_kernel(n_tile, row_ref, exp_ref, wide_ref, *picks):
     for level in range(row_ref.shape[0]):
         for j in range(row_ref.shape[1]):
             wide_ref[level, j] = wide_of(row_ref[level, j])
-
-
-def expand_weights_kernel(n_tile, exp_ref, other_ref, last_ref):
     box, _, leaf = exp_ref.shape
     tile = lax.axis_index("tile")
     relative, out_rows, unit, pieces = slots_of(n_tile, box, leaf)
-    for slot in range(n_tile // 2):
+    group = n_tile // 4
+    for slot in range(n_tile):
         block = tile ^ relative[slot]
         for piece in range(pieces):
             n = (block * out_rows + piece * unit) // leaf
-            both = jnp.concatenate([exp_ref[n], other_ref[n]], axis=0).T
+            picks[slot // group][slot % group * pieces + piece] = exp_ref[n]
+
+
+def expand_weights_kernel(n_tile, *refs):
+    ins, last_ref = refs[:-1], refs[-1]
+    count, _, leaf = ins[0].shape
+    unit = last_ref.shape[2]
+    tile = lax.axis_index("tile")
+    relative = slots_of(n_tile, 1, leaf)[0]
+    for k in range(count):
+        block = tile ^ relative[k * n_tile // 4 // count]
+        for part in range(2):
+            both = jnp.concatenate([ins[2 * part][k], ins[2 * part + 1][k]], axis=0).T
             rows = both[:unit]
-            for k in range(1, leaf // unit):
-                rows = jnp.where(block % (leaf // unit) == k, both[k * unit:(k + 1) * unit], rows)
-            last_ref[slot * pieces + piece] = wide_of(rows)
+            for at in range(1, leaf // unit):
+                rows = jnp.where(block % (leaf // unit) == at, both[at * unit:(at + 1) * unit], rows)
+            last_ref[part, k] = wide_of(rows)
 
 
 def row_kernel(n_seg, n_tile, leaf, *refs):
@@ -180,14 +191,20 @@
             outs[slot // group][at:at + rank, :] = full[pl.ds(pl.multiple_of(n * rank, rank), rank), :]
 
 
-def expand_kernel(part, own_ref, other_ref, last_ref, out_ref):
-    rank = last_ref.shape[2] // 4
-    unit = last_ref.shape[1]
-    for k in range(own_ref.shape[0] // rank):
+def expand_kernel(part, *refs):
+    own_ref, other_ref, last_ref = refs[part:part + 3]
+    outs = refs[part + 3:]
+    count, unit = last_ref.shape[1:3]
+    rank = last_ref.shape[3] // 4
+    for k in range(count):
         rows = slice(k * rank, (k + 1) * rank)
         v = jnp.concatenate([own_ref[rows, :], other_ref[rows, :]], axis=0)
-        wide = last_ref[part * own_ref.shape[0] // rank + k]
-        out_ref[k * unit:(k + 1) * unit, :] = product3(wide, *split(v))
+        out = product3(last_ref[part, k], *split(v))
+        if part:
+            out = out + refs[0][k * unit:(k + 1) * unit, :]
+        at = k * unit * len(outs)
+        target, at = outs[at // (count * unit)], at % (count * unit) // len(outs)
+        target[at:at + unit, :] = out
 
 
 def tie(x, *others):
@@ -204,6 +221,7 @@
     bits = n_tile.bit_length() - 1
     part = jax.ShapeDtypeStruct((box * rank // n_seg, CHUNK), F32)
     quarter = jax.ShapeDtypeStruct((n_tile // 4 * pieces * rank, CHUNK), F32)
+    eighth = jax.ShapeDtypeStruct((box * leaf // 8, CHUNK), F32)
     summed = jax.ShapeDtypeStruct((box * leaf // 4, CHUNK), F32)
     params = pltpu.CompilerParams(vmem_limit_bytes=16 * 2**20)
     cost = pl.CostEstimate(flops=1_000_000, bytes_accessed=100_000, transcendentals=0)
@@ -234,26 +252,27 @@
         return [outs[k * n_seg:(k + 1) * n_seg] for k in range(count)]
 
     def row_weights():
+        pick = jax.ShapeDtypeStruct((n_tile // 4 * pieces, rank, leaf), F32)
         return pl.pallas_call(
-            weights_kernel,
-            in_specs=[in_vmem],
-            out_specs=in_vmem,
-            out_shape=jax.ShapeDtypeStruct((levels, pairs, 2 * rank, 4 * rank), BF16),
+            functools.partial(weights_kernel, n_tile),
+            in_specs=[in_vmem] * 2,
+            out_specs=[in_vmem] * 5,
+            out_shape=[jax.ShapeDtypeStruct((levels, pairs, 2 * rank, 4 * rank), BF16)] + [pick] * 4,
             compiler_params=params,
             cost_estimate=cost,
             name="row_weights",
-        )(row)
-
-    def expand_weights(other):
+        )(row, expand)
+
+    def expand_weights(*tiles):
         return pl.pallas_call(
             functools.partial(expand_weights_kernel, n_tile),
-            in_specs=[in_vmem] * 2,
+            in_specs=[in_vmem] * 4,
             out_specs=in_vmem,
-            out_shape=jax.ShapeDtypeStruct((n_tile // 2 * pieces, unit, 4 * rank), BF16),
+            out_shape=jax.ShapeDtypeStruct((2, n_tile // 4 * pieces, unit, 4 * rank), BF16),
             compiler_params=params,
             cost_estimate=cost,
             name="expand_weights",
-        )(expand, other)
+        )(*tiles)
 
     def row_side(parts, wide):
         return pl.pallas_call(
@@ -267,16 +286,16 @@
             name="row_side",
         )(*parts, wide)
 
-    def expanded(part, own, other, last):
+    def expanded(part, *operands):
         return pl.pallas_call(
             functools.partial(expand_kernel, part),
-            in_specs=[in_vmem] * 3,
-            out_specs=in_vmem,
-            out_shape=summed,
+            in_specs=[in_vmem] * (3 + part),
+            out_specs=[in_vmem] * (1 + part),
+            out_shape=[eighth] * 2 if part else [summed],
             compiler_params=params,
-            cost_estimate=pl.CostEstimate(flops=(1 - part) * 2_000_000_000 + 1, bytes_accessed=100_000, transcendentals=0),
+            cost_estimate=pl.CostEstimate(flops=LOW, bytes_accessed=100_000, transcendentals=0),
             name="expand",
-        )(own, other, last)
+        )(*operands)
 
     def swap(x, axis, size, mask):
         return lax.ppermute(x, axis, [(i, i ^ mask) for i in range(size)])
@@ -295,53 +314,41 @@
     received = {0: exchange(parts[0])}
     parts += column_side(1, chunks - 1, tie(mid, parts[0][-1]), 52)
     received[1] = exchange(parts[1])
-    wide = row_weights()
-    last_wide = expand_weights(swap(tie(expand, wide), "tile", n_tile, 1))
-
-    terms, sends, lows = [], {}, []
+    wide, *picks = row_weights()
+    last_wide = expand_weights(picks[0], *[swap(picks[k], "tile", n_tile, m) for k, m in ((2, 1), (1, 2), (3, 3))])
+
+    terms, sends = [], {}
     last = chunks - 1
 
-    def forward(group, b, *after):
-        for c in group:
+    def forward(c, b, *after):
+        if b == 2:
+            near, own, other = terms[c]
+            low, send = expanded(1, near, tie(own, *after), other, last_wide)
+            terms[c] = [low]
+        else:
             terms[c][-1] = tie(terms[c][-1], *after)
-        send = jnp.concatenate([next_send(terms[c]) for c in group])
-        sends[group[-1], b] = send
-        got = swap(send, "tile", n_tile, 1 << b)
-        rows = got.shape[0] // len(group)
-        for k, c in enumerate(group):
-            terms[c].append(got[k * rows:(k + 1) * rows])
+            send = next_send(terms[c])
+        sends[c, b] = send
+        terms[c].append(swap(send, "tile", n_tile, 1 << b))
         return send
 
-    def low_half(c, *after):
-        own, other = lows[c]
-        terms[c][0] = expanded(0, own, tie(other, *after), last_wide)
-        return terms[c][0]
-
-    early = list(range(last - 1))
     for c in range(chunks):
-        after = [sends[c - 1, 1]] if c else [parts[-1][0]]
-        if c == last:
-            after.append(forward(early, 2, sends[c - 1, 1]))
-        own_low, own_high, low, high = row_side([tie(x, *after) for x in received[c]], wide)
-        lows.append((own_low, swap(low, "tile", n_tile, 1)))
-        done = []
-        if c >= 1:
-            done.append(low_half(c - 1, own_high))
-        got = swap(high, "tile", n_tile, 1)
-        if done:
-            got = tie(got, *done)
-        sends[c, 1] = expanded(1, own_high, got, last_wide)
-        terms.append([None, swap(sends[c, 1], "tile", n_tile, 2)])
+        after = terms[c - 1][0] if c else parts[-1][0]
+        own, to_y, to_core, to_both = row_side([tie(x, after) for x in received[c]], wide)
+        from_core = swap(to_core, "tile", n_tile, 1)
+        if c:
+            from_core = tie(from_core, forward(c - 1, 2, own))
+        near = expanded(0, own, from_core, last_wide)[0]
+        terms.append([near, swap(to_y, "tile", n_tile, 2), swap(to_both, "tile", n_tile, 3)])
         if c + 2 < chunks:
-            received[c + 2] = exchange(parts[c + 2], own_high)
-    low_half(last, sends[last, 1])
-    done = sends[last, 1]
-    for group, b in ((early, 3), ([last - 1], 2), ([last], 2), ([last - 1], 3), ([last], 3)):
+            received[c + 2] = exchange(parts[c + 2], own)
+    done = terms[last][0]
+    for c, b in [(k, 3) for k in range(last - 1)] + [(last, 2), (last - 1, 3), (last, 3)]:
         if b < bits:
-            done = forward(group, b, done)
+            done = forward(c, b, done)
     for b in range(4, bits):
-        for group in (early, [last - 1], [last]):
-            done = forward(group, b, done)
+        for c in range(chunks):
+            done = forward(c, b, done)
     return jnp.concatenate([total(t, 0, out_rows) for t in terms], axis=1)
 
 

time: 60.4 us -> 66.7 us (1.10)
  starting transfers between devices: 21.5 us -> 30.3 us
  waiting for transfers between devices: 20.2 us -> 18.7 us
  local copies, waits for them, and re-layouts: 0.81 us -> 0.01 us
    ppermute x23 -> x27, starting transfers between devices: 21.5 us -> 30.3 us  [swap(): return lax.ppermute(x, axis, [(i, i ^ mask) for i in range(size)])]
    ppermute x23 -> x27, waiting for transfers between devices: 20.2 us -> 18.7 us  [swap(): return lax.ppermute(x, axis, [(i, i ^ mask) for i in range(size)])]
    unnamed x4, local copies, waits for them, and re-layouts: 0.79 us -> 0.01 us
  transfers between devices with their start and end apart: 23 -> 27, of which waited for: 11 -> 11; matrix products, arithmetic and copies ran while one was open for 0% -> 0% of each run, Pallas kernels for 21% -> 19%
where the time goes in v3:
time: 66.7 us; the launch traced here: 66.6 us
  starting transfers between devices  30.3 us (45%)
  waiting for transfers between devices  18.7 us (28%)
  Pallas kernels  16.6 us (25%)
  other arithmetic  0.81 us (1%)
    ppermute x27, starting transfers between devices, swap(): return lax.ppermute(x, axis, [(i, i ^ mask) for i in range(size)])  30.3 us
    ppermute x27, waiting for transfers between devices, swap(): return lax.ppermute(x, axis, [(i, i ^ mask) for i in range(size)])  18.7 us
    pallas_call x2, Pallas kernels, column_side(): pl.pallas_call(functools.partial(column_kernel, n_seg, pieces, start * CH...  9.5 us
    pallas_call x4, Pallas kernels, row_side(): pl.pallas_call(functools.partial(row_kernel, n_seg, n_tile, leaf), in_spe...  4.72 us
    pallas_call x8, Pallas kernels, expanded(): pl.pallas_call(functools.partial(expand_kernel, part), in_specs=[in_vmem]...  1.9 us
  transfers between devices with their start and end apart: 27, of which 11 were waited for; matrix products, arithmetic and copies ran while one was open for 0% of the time, Pallas kernels for 19%

profile of v3, /device:TPU:0, one launch (start us, length us, event | category | flops | bytes accessed | tf_op | source)
XLA Modules:
  0.0 66.6 jit_solution(2600181777042663284)
XLA Ops:
  0.0 3.7 %column_side.2 = (f32[512,128]{1,0:T(8,128)S(1)}, f32[512,128]{1,0:T(8,128)S(1)}) custom-call(f32[2048,512]{1,0:T(8,128)} %x_hbm.3, f32[16,64,128]{2,1,0:T(8,128)} %bitcast.11, f32[4,8,128,128]{3,2,1,0:T(8,128)} %bitcast.9, f32[16,64,64]{2,1,0:T(8,128)} %bitcast.13), custom_call_target="tpu_custom_call" | custom-call | flops 1000000 | bytes 100000 | tf_op jit(solution)/shard_map/column_side/pallas_call | solution.py:234
  3.7 0.0 copy-start
  3.7 0.0 copy-start.1
  3.7 3.0 %collective-permute-start = (f32[512,128]{1,0:T(8,128)S(1)}, f32[512,128]{1,0:T(8,128)S(1)}, u32[]{:S(2)}, u32[]{:S(2)}) collective-permute-start(f32[512,128]{1,0:T(8,128)S(1)} %get-tuple-element.65), channel_id=1, source_target_pairs={{0,1},{1,0},{2,3},{3,2},{4,5},{5,4},{6,7},{7,6},{8,9},{9,8},{10,11... | collective-permute-start | bytes 786440 | tf_op jit(solution)/shard_map/ppermute | solution.py:301
  6.7 5.8 %column_side.3 = (f32[512,128]{1,0:T(8,128)S(1)}, f32[512,128]{1,0:T(8,128)S(1)}, f32[512,128]{1,0:T(8,128)S(1)}, f32[512,128]{1,0:T(8,128)S(1)}, f32[512,128]{1,0:T(8,128)S(1)}, /*index=5*/f32[512,128]{1,0:T(8,128)S(1)}) custom-call(f32[2048,512]{1,0:T(8,128)} %x_hbm.3, f32[16,64,128]{2,1,0:T(8,128)} %bitcast.12, f32[4,8,128,128]{3,2,1,0:T(8,128)} %bitcast.10, ...), custom_call_target="tpu_custom_call" | custom-call | flops 1000000 | bytes 100000 | tf_op jit(solution)/shard_map/column_side/pallas_call | solution.py:234
  12.5 0.2 collective-permute-start.6
  12.8 0.3 row_weights.1
  13.0 0.1 collective-permute-start.2
  13.1 2.1 %collective-permute-start.3 = (f32[4,64,128]{2,1,0:T(8,128)S(1)}, f32[4,64,128]{2,1,0:T(8,128)S(1)}, u32[]{:S(2)}, u32[]{:S(2)}) collective-permute-start(f32[4,64,128]{2,1,0:T(8,128)S(1)} %get-tuple-element.75), channel_id=1, source_target_pairs={{0,4},{2,6},{4,0},{6,2},{8,12},{10,14},{12,8},{14,10},{16,20},{18,... | collective-permute-start | bytes 393224 | tf_op jit(solution)/shard_map/ppermute | solution.py:301
  15.2 0.1 collective-permute-start.4
  15.3 0.0 collective-permute-done.refs_1_
  15.3 1.2 %row_side.4 = (f32[256,128]{1,0:T(8,128)S(1)}, f32[256,128]{1,0:T(8,128)S(1)}, f32[256,128]{1,0:T(8,128)S(1)}, f32[256,128]{1,0:T(8,128)S(1)}) custom-call(f32[512,128]{1,0:T(8,128)S(1)} %get-tuple-element.68.refs_0_, f32[512,128]{1,0:T(8,128)S(1)} %collective-permute-done.refs_1_, bf16[4,8,128,256]{3,2,1,0:T(8,128)(2,1)S(1)} %get-tuple-element.70.refs_2_), custom_call_target="tpu_custom_call" | custom-call | flops 20000000000 | bytes 100000 | tf_op jit(solution)/shard_map/row_side/pallas_call | solution.py:278
  16.5 0.2 collective-permute-start.1
  16.7 0.0 collective-permute-done.2.refs_1_
  16.7 2.9 %collective-permute-done.3.refs_2_ = f32[4,64,128]{2,1,0:T(8,128)S(1)} collective-permute-done((f32[4,64,128]{2,1,0:T(8,128)S(1)}, f32[4,64,128]{2,1,0:T(8,128)S(1)}, u32[]{:S(2)}, u32[]{:S(2)}) %collective-permute-start.3) | collective-permute-done | bytes 131104 | tf_op jit(solution)/shard_map/ppermute | solution.py:301
  19.6 2.3 %collective-permute-done.4.refs_3_ = f32[4,64,128]{2,1,0:T(8,128)S(1)} collective-permute-done((f32[4,64,128]{2,1,0:T(8,128)S(1)}, f32[4,64,128]{2,1,0:T(8,128)S(1)}, u32[]{:S(2)}, u32[]{:S(2)}) %collective-permute-start.4) | collective-permute-done | bytes 131104 | tf_op jit(solution)/shard_map/ppermute | solution.py:301
  21.9 0.2 expand_weights.1.refs_2_.refs_3_
  22.1 1.6 %collective-permute-start.5 = (f32[256,128]{1,0:T(8,128)S(1)}, f32[256,128]{1,0:T(8,128)S(1)}, u32[]{:S(2)}, u32[]{:S(2)}) collective-permute-start(f32[256,128]{1,0:T(8,128)S(1)} %get-tuple-element.77), channel_id=1, source_target_pairs={{0,4},{2,6},{4,0},{6,2},{8,12},{10,14},{12,8},{14,10},{16,20},{18,... | collective-permute-start | bytes 393224 | tf_op jit(solution)/shard_map/ppermute | solution.py:301
  23.7 1.4 %collective-permute-start.10 = (f32[512,128]{1,0:T(8,128)S(1)}, f32[512,128]{1,0:T(8,128)S(1)}, u32[]{:S(2)}, u32[]{:S(2)}) collective-permute-start(f32[512,128]{1,0:T(8,128)S(1)} %get-tuple-element.92), channel_id=1, source_target_pairs={{0,1},{1,0},{2,3},{3,2},{4,5},{5,4},{6,7},{7,6},{8,9},{9,8},{10,11... | collective-permute-start | bytes 786440 | tf_op jit(solution)/shard_map/ppermute | solution.py:301
  25.2 0.0 collective-permute-done.1.refs_1_
  25.2 0.2 expand.8.refs_0_
  25.4 1.2 %row_side.5 = (f32[256,128]{1,0:T(8,128)S(1)}, f32[256,128]{1,0:T(8,128)S(1)}, f32[256,128]{1,0:T(8,128)S(1)}, f32[256,128]{1,0:T(8,128)S(1)}) custom-call(f32[512,128]{1,0:T(8,128)S(1)} %get-tuple-element.79.refs_0_, f32[512,128]{1,0:T(8,128)S(1)} %collective-permute-done.6.refs_1_, bf16[4,8,128,256]{3,2,1,0:T(8,128)(2,1)S(1)} %get-tuple-element.70.refs_2_), custom_call_target="tpu_custom_call" | custom-call | flops 20000000000 | bytes 100000 | tf_op jit(solution)/shard_map/row_side/pallas_call | solution.py:278
  26.6 0.3 collective-permute-start.9
  26.9 1.6 %collective-permute-done.5.refs_1_ = f32[256,128]{1,0:T(8,128)S(1)} collective-permute-done((f32[256,128]{1,0:T(8,128)S(1)}, f32[256,128]{1,0:T(8,128)S(1)}, u32[]{:S(2)}, u32[]{:S(2)}) %collective-permute-start.5) | collective-permute-done | bytes 131104 | tf_op jit(solution)/shard_map/ppermute | solution.py:301
  28.5 1.5 %collective-permute-start.12 = (f32[256,128]{1,0:T(8,128)S(1)}, f32[256,128]{1,0:T(8,128)S(1)}, u32[]{:S(2)}, u32[]{:S(2)}) collective-permute-start(f32[256,128]{1,0:T(8,128)S(1)} %get-tuple-element.96), channel_id=1, source_target_pairs={{0,4},{2,6},{4,0},{6,2},{8,12},{10,14},{12,8},{14,10},{16,20},{18,... | collective-permute-start | bytes 393224 | tf_op jit(solution)/shard_map/ppermute | solution.py:301
  30.0 0.0 collective-permute-start.13
  30.1 0.3 collective-permute-done.7.refs_2_
  30.4 1.3 %collective-permute-start.14 = (f32[512,128]{1,0:T(8,128)S(1)}, f32[512,128]{1,0:T(8,128)S(1)}, u32[]{:S(2)}, u32[]{:S(2)}) collective-permute-start(f32[512,128]{1,0:T(8,128)S(1)} %get-tuple-element.103), channel_id=1, source_target_pairs={{0,1},{1,0},{2,3},{3,2},{4,5},{5,4},{6,7},{7,6},{8,9},{9,8},{10,11... | collective-permute-start | bytes 786440 | tf_op jit(solution)/shard_map/ppermute | solution.py:301
  31.7 0.2 expand.9
  32.0 0.2 expand.10.refs_0_
  32.2 0.3 collective-permute-done.10.refs_1_
  32.5 1.2 %row_side.6 = (f32[256,128]{1,0:T(8,128)S(1)}, f32[256,128]{1,0:T(8,128)S(1)}, f32[256,128]{1,0:T(8,128)S(1)}, f32[256,128]{1,0:T(8,128)S(1)}) custom-call(f32[512,128]{1,0:T(8,128)S(1)} %get-tuple-element.90.refs_0_, f32[512,128]{1,0:T(8,128)S(1)} %collective-permute-done.10.refs_1_, bf16[4,8,128,256]{3,2,1,0:T(8,128)(2,1)S(1)} %get-tuple-element.70.refs_2_), custom_call_target="tpu_custom_call" | custom-call | flops 20000000000 | bytes 100000 | tf_op jit(solution)/shard_map/row_side/pallas_call | solution.py:278
  33.7 0.6 collective-permute-start.11
  34.3 2.1 %collective-permute-start.16 = (f32[256,128]{1,0:T(8,128)S(1)}, f32[256,128]{1,0:T(8,128)S(1)}, u32[]{:S(2)}, u32[]{:S(2)}) collective-permute-start(f32[256,128]{1,0:T(8,128)S(1)} %get-tuple-element.107), channel_id=1, source_target_pairs={{0,4},{2,6},{4,0},{6,2},{8,12},{10,14},{12,8},{14,10},{16,20},{18,... | collective-permute-start | bytes 393224 | tf_op jit(solution)/shard_map/ppermute | solution.py:301
  36.4 0.0 collective-permute-start.17
  36.4 0.2 expand.11
  36.7 0.2 expand.12.refs_0_
  36.9 2.5 %collective-permute-done.14.refs_1_ = f32[512,128]{1,0:T(8,128)S(1)} collective-permute-done((f32[512,128]{1,0:T(8,128)S(1)}, f32[512,128]{1,0:T(8,128)S(1)}, u32[]{:S(2)}, u32[]{:S(2)}) %collective-permute-start.14) | collective-permute-done | bytes 262176 | tf_op jit(solution)/shard_map/ppermute | solution.py:301
  39.4 1.2 %row_side.7 = (f32[256,128]{1,0:T(8,128)S(1)}, f32[256,128]{1,0:T(8,128)S(1)}, f32[256,128]{1,0:T(8,128)S(1)}, f32[256,128]{1,0:T(8,128)S(1)}) custom-call(f32[512,128]{1,0:T(8,128)S(1)} %get-tuple-element.101.refs_0_, f32[512,128]{1,0:T(8,128)S(1)} %collective-permute-done.14.refs_1_, bf16[4,8,128,256]{3,2,1,0:T(8,128)(2,1)S(1)} %get-tuple-element.70.refs_2_), custom_call_target="tpu_custom_call" | custom-call | flops 20000000000 | bytes 100000 | tf_op jit(solution)/shard_map/row_side/pallas_call | solution.py:278
  40.6 0.1 collective-permute-start.15
  40.7 1.8 %collective-permute-start.8 = (f32[256,128]{1,0:T(8,128)S(1)}, f32[256,128]{1,0:T(8,128)S(1)}, u32[]{:S(2)}, u32[]{:S(2)}) collective-permute-start(f32[256,128]{1,0:T(8,128)S(1)} %get-tuple-element.86), channel_id=1, source_target_pairs={{0,8},{2,10},{4,12},{6,14},{8,0},{10,2},{12,4},{14,6},{16,24},{18,... | collective-permute-start | bytes 393224 | tf_op jit(solution)/shard_map/ppermute | solution.py:301
  42.5 0.3 collective-permute-start.19
  42.8 1.3 %collective-permute-start.22 = (f32[256,128]{1,0:T(8,128)S(1)}, f32[256,128]{1,0:T(8,128)S(1)}, u32[]{:S(2)}, u32[]{:S(2)}) collective-permute-start(f32[256,128]{1,0:T(8,128)S(1)} %get-tuple-element.116), channel_id=1, source_target_pairs={{0,4},{2,6},{4,0},{6,2},{8,12},{10,14},{12,8},{14,10},{16,20},{18,... | collective-permute-start | bytes 393224 | tf_op jit(solution)/shard_map/ppermute | solution.py:301
  44.1 0.0 collective-permute-done.17.refs_2_
  44.1 0.0 collective-permute-start.23
  44.1 0.2 expand.13
  44.4 0.0 collective-permute-done.15.refs_1_
  44.4 1.6 %collective-permute-start.21 = (f32[256,128]{1,0:T(8,128)S(1)}, f32[256,128]{1,0:T(8,128)S(1)}, u32[]{:S(2)}, u32[]{:S(2)}) collective-permute-start(f32[256,128]{1,0:T(8,128)S(1)} %get-tuple-element.110), channel_id=1, source_target_pairs={{0,8},{2,10},{4,12},{6,14},{8,0},{10,2},{12,4},{14,6},{16,24},{18,... | collective-permute-start | bytes 393224 | tf_op jit(solution)/shard_map/ppermute | solution.py:301
  46.0 0.2 expand.14.refs_0_
  46.3 0.8 %collective-permute-done.8 = f32[256,128]{1,0:T(8,128)S(1)} collective-permute-done((f32[256,128]{1,0:T(8,128)S(1)}, f32[256,128]{1,0:T(8,128)S(1)}, u32[]{:S(2)}, u32[]{:S(2)}) %collective-permute-start.8) | collective-permute-done | bytes 131104 | tf_op jit(solution)/shard_map/ppermute | solution.py:301
  47.1 2.8 %collective-permute-start.18 = (f32[128,128]{1,0:T(8,128)S(1)}, f32[128,128]{1,0:T(8,128)S(1)}, u32[]{:S(2)}, u32[]{:S(2)}) collective-permute-start(f32[128,128]{1,0:T(8,128)S(1)} %slice_add_fusion.3), channel_id=1, source_target_pairs={{0,16},{2,18},{4,20},{6,22},{8,24},{10,26},{12,28},{14,30},{16,0},... | collective-permute-start | bytes 196616 | tf_op jit(solution)/shard_map/ppermute | solution.py:301
  49.9 0.0 collective-permute-done.19
  49.9 2.8 %collective-permute-start.20 = (f32[128,128]{1,0:T(8,128)S(1)}, f32[128,128]{1,0:T(8,128)S(1)}, u32[]{:S(2)}, u32[]{:S(2)}) collective-permute-start(f32[128,128]{1,0:T(8,128)S(1)} %slice_add_fusion.2), channel_id=1, source_target_pairs={{0,16},{2,18},{4,20},{6,22},{8,24},{10,26},{12,28},{14,30},{16,0},... | collective-permute-start | bytes 196616 | tf_op jit(solution)/shard_map/ppermute | solution.py:301
  52.7 0.0 collective-permute-done.22.refs_1_
  52.7 0.0 collective-permute-done.23.refs_2_
  52.7 0.2 expand.15
  53.0 2.3 %collective-permute-start.25 = (f32[256,128]{1,0:T(8,128)S(1)}, f32[256,128]{1,0:T(8,128)S(1)}, u32[]{:S(2)}, u32[]{:S(2)}) collective-permute-start(f32[256,128]{1,0:T(8,128)S(1)} %get-tuple-element.119), channel_id=1, source_target_pairs={{0,8},{2,10},{4,12},{6,14},{8,0},{10,2},{12,4},{14,6},{16,24},{18,... | collective-permute-start | bytes 393224 | tf_op jit(solution)/shard_map/ppermute | solution.py:301
  55.3 0.2 collective-permute-start.24
  55.5 1.8 %collective-permute-done.20 = f32[128,128]{1,0:T(8,128)S(1)} collective-permute-done((f32[128,128]{1,0:T(8,128)S(1)}, f32[128,128]{1,0:T(8,128)S(1)}, u32[]{:S(2)}, u32[]{:S(2)}) %collective-permute-start.20) | collective-permute-done | bytes 65568 | tf_op jit(solution)/shard_map/ppermute | solution.py:301
  57.4 1.8 %collective-permute-done.25 = f32[256,128]{1,0:T(8,128)S(1)} collective-permute-done((f32[256,128]{1,0:T(8,128)S(1)}, f32[256,128]{1,0:T(8,128)S(1)}, u32[]{:S(2)}, u32[]{:S(2)}) %collective-permute-start.25) | collective-permute-done | bytes 131104 | tf_op jit(solution)/shard_map/ppermute | solution.py:301
  59.2 2.3 %collective-permute-start.26 = (f32[128,128]{1,0:T(8,128)S(1)}, f32[128,128]{1,0:T(8,128)S(1)}, u32[]{:S(2)}, u32[]{:S(2)}) collective-permute-start(f32[128,128]{1,0:T(8,128)S(1)} %slice_add_fusion), channel_id=1, source_target_pairs={{0,16},{2,18},{4,20},{6,22},{8,24},{10,26},{12,28},{14,30},{16,0},... | collective-permute-start | bytes 196616 | tf_op jit(solution)/shard_map/ppermute | solution.py:301
  61.5 0.2 collective-permute-done.24
  61.7 4.2 %collective-permute-done.26 = f32[128,128]{1,0:T(8,128)S(1)} collective-permute-done((f32[128,128]{1,0:T(8,128)S(1)}, f32[128,128]{1,0:T(8,128)S(1)}, u32[]{:S(2)}, u32[]{:S(2)}) %collective-permute-start.26) | collective-permute-done | bytes 65568 | tf_op jit(solution)/shard_map/ppermute | solution.py:301
  65.9 0.7 %pad_maximum_fusion = f32[128,512]{1,0:T(8,128)} fusion(f32[128,128]{1,0:T(8,128)S(1)} %add_add_fusion, f32[128,128]{1,0:T(8,128)S(1)} %add_add_fusion.1, f32[128,128]{1,0:T(8,128)S(1)} %add_add_fusion.2, f32[128,128]{1,0:T(8,128)S(1)} %add_add_fusion.3), kind=kLoop, calls=%fused_computation | loop fusion | flops 196608 | bytes 524288 | tf_op jit(solution)/shard_map/concatenate | solution.py:352
  (19 shorter events, 0.1 us)
Async XLA Ops:
  3.7 9.1 %copy-start = (f32[1,4,8,128,128]{4,3,2,1,0:T(8,128)S(1)}, f32[1,4,8,128,128]{4,3,2,1,0:T(8,128)}, u32[]{:S(2)}) copy-start(f32[1,4,8,128,128]{4,3,2,1,0:T(8,128)} %param.10) | copy-start | bytes 6291460
  3.7 9.1 %copy-start.1 = (f32[1,16,128,64]{2,3,1,0:T(8,128)S(1)}, f32[1,16,128,64]{2,3,1,0:T(8,128)}, u32[]{:S(2)}) copy-start(f32[1,16,128,64]{2,3,1,0:T(8,128)} %param.11) | copy-start | bytes 1572868
  3.7 11.6 %collective-permute-start = (f32[512,128]{1,0:T(8,128)S(1)}, f32[512,128]{1,0:T(8,128)S(1)}, u32[]{:S(2)}, u32[]{:S(2)}) collective-permute-start(f32[512,128]{1,0:T(8,128)S(1)} %get-tuple-element.65), channel_id=1, source_target_pairs={{0,1},{1,0},{2,3},{3,2},{4,5},{5,4},{6,7},{7,6},{8,9},{9,8},{10,11... | collective-permute-start | bytes 786440 | tf_op jit(solution)/shard_map/ppermute | solution.py:301
  12.5 12.9 %collective-permute-start.6 = (f32[512,128]{1,0:T(8,128)S(1)}, f32[512,128]{1,0:T(8,128)S(1)}, u32[]{:S(2)}, u32[]{:S(2)}) collective-permute-start(f32[512,128]{1,0:T(8,128)S(1)} %get-tuple-element.80), channel_id=1, source_target_pairs={{0,1},{1,0},{2,3},{3,2},{4,5},{5,4},{6,7},{7,6},{8,9},{9,8},{10,11... | collective-permute-start | bytes 786440 | tf_op jit(solution)/shard_map/ppermute | solution.py:301
  13.0 3.7 %collective-permute-start.2 = (f32[4,64,128]{2,1,0:T(8,128)S(1)}, f32[4,64,128]{2,1,0:T(8,128)S(1)}, u32[]{:S(2)}, u32[]{:S(2)}) collective-permute-start(f32[4,64,128]{2,1,0:T(8,128)S(1)} %get-tuple-element.74), channel_id=1, source_target_pairs={{0,2},{2,0},{4,6},{6,4},{8,10},{10,8},{12,14},{14,12},{16,18},{18,... | collective-permute-start | bytes 393224 | tf_op jit(solution)/shard_map/ppermute | solution.py:301
  13.1 6.5 %collective-permute-start.3 = (f32[4,64,128]{2,1,0:T(8,128)S(1)}, f32[4,64,128]{2,1,0:T(8,128)S(1)}, u32[]{:S(2)}, u32[]{:S(2)}) collective-permute-start(f32[4,64,128]{2,1,0:T(8,128)S(1)} %get-tuple-element.75), channel_id=1, source_target_pairs={{0,4},{2,6},{4,0},{6,2},{8,12},{10,14},{12,8},{14,10},{16,20},{18,... | collective-permute-start | bytes 393224 | tf_op jit(solution)/shard_map/ppermute | solution.py:301
  15.2 6.6 %collective-permute-start.4 = (f32[4,64,128]{2,1,0:T(8,128)S(1)}, f32[4,64,128]{2,1,0:T(8,128)S(1)}, u32[]{:S(2)}, u32[]{:S(2)}) collective-permute-start(f32[4,64,128]{2,1,0:T(8,128)S(1)} %get-tuple-element.76), channel_id=1, source_target_pairs={{0,6},{2,4},{4,2},{6,0},{8,14},{10,12},{12,10},{14,8},{16,22},{18,... | collective-permute-start | bytes 393224 | tf_op jit(solution)/shard_map/ppermute | solution.py:301
  16.5 8.7 %collective-permute-start.1 = (f32[256,128]{1,0:T(8,128)S(1)}, f32[256,128]{1,0:T(8,128)S(1)}, u32[]{:S(2)}, u32[]{:S(2)}) collective-permute-start(f32[256,128]{1,0:T(8,128)S(1)} %get-tuple-element.72), channel_id=1, source_target_pairs={{0,2},{2,0},{4,6},{6,4},{8,10},{10,8},{12,14},{14,12},{16,18},{18,... | collective-permute-start | bytes 393224 | tf_op jit(solution)/shard_map/ppermute | solution.py:301
  22.1 6.4 %collective-permute-start.5 = (f32[256,128]{1,0:T(8,128)S(1)}, f32[256,128]{1,0:T(8,128)S(1)}, u32[]{:S(2)}, u32[]{:S(2)}) collective-permute-start(f32[256,128]{1,0:T(8,128)S(1)} %get-tuple-element.77), channel_id=1, source_target_pairs={{0,4},{2,6},{4,0},{6,2},{8,12},{10,14},{12,8},{14,10},{16,20},{18,... | collective-permute-start | bytes 393224 | tf_op jit(solution)/shard_map/ppermute | solution.py:301
  23.7 6.7 %collective-permute-start.7 = (f32[256,128]{1,0:T(8,128)S(1)}, f32[256,128]{1,0:T(8,128)S(1)}, u32[]{:S(2)}, u32[]{:S(2)}) collective-permute-start(f32[256,128]{1,0:T(8,128)S(1)} %get-tuple-element.84), channel_id=1, source_target_pairs={{0,6},{2,4},{4,2},{6,0},{8,14},{10,12},{12,10},{14,8},{16,22},{18,... | collective-permute-start | bytes 393224 | tf_op jit(solution)/shard_map/ppermute | solution.py:301
  23.7 8.8 %collective-permute-start.10 = (f32[512,128]{1,0:T(8,128)S(1)}, f32[512,128]{1,0:T(8,128)S(1)}, u32[]{:S(2)}, u32[]{:S(2)}) collective-permute-start(f32[512,128]{1,0:T(8,128)S(1)} %get-tuple-element.92), channel_id=1, source_target_pairs={{0,1},{1,0},{2,3},{3,2},{4,5},{5,4},{6,7},{7,6},{8,9},{9,8},{10,11... | collective-permute-start | bytes 786440 | tf_op jit(solution)/shard_map/ppermute | solution.py:301
  26.6 5.3 %collective-permute-start.9 = (f32[256,128]{1,0:T(8,128)S(1)}, f32[256,128]{1,0:T(8,128)S(1)}, u32[]{:S(2)}, u32[]{:S(2)}) collective-permute-start(f32[256,128]{1,0:T(8,128)S(1)} %get-tuple-element.88), channel_id=1, source_target_pairs={{0,2},{2,0},{4,6},{6,4},{8,10},{10,8},{12,14},{14,12},{16,18},{18,... | collective-permute-start | bytes 393224 | tf_op jit(solution)/shard_map/ppermute | solution.py:301
  28.5 5.8 %collective-permute-start.12 = (f32[256,128]{1,0:T(8,128)S(1)}, f32[256,128]{1,0:T(8,128)S(1)}, u32[]{:S(2)}, u32[]{:S(2)}) collective-permute-start(f32[256,128]{1,0:T(8,128)S(1)} %get-tuple-element.96), channel_id=1, source_target_pairs={{0,4},{2,6},{4,0},{6,2},{8,12},{10,14},{12,8},{14,10},{16,20},{18,... | collective-permute-start | bytes 393224 | tf_op jit(solution)/shard_map/ppermute | solution.py:301
  30.0 6.4 %collective-permute-start.13 = (f32[256,128]{1,0:T(8,128)S(1)}, f32[256,128]{1,0:T(8,128)S(1)}, u32[]{:S(2)}, u32[]{:S(2)}) collective-permute-start(f32[256,128]{1,0:T(8,128)S(1)} %get-tuple-element.98), channel_id=1, source_target_pairs={{0,6},{2,4},{4,2},{6,0},{8,14},{10,12},{12,10},{14,8},{16,22},{18,... | collective-permute-start | bytes 393224 | tf_op jit(solution)/shard_map/ppermute | solution.py:301
  30.4 9.1 %collective-permute-start.14 = (f32[512,128]{1,0:T(8,128)S(1)}, f32[512,128]{1,0:T(8,128)S(1)}, u32[]{:S(2)}, u32[]{:S(2)}) collective-permute-start(f32[512,128]{1,0:T(8,128)S(1)} %get-tuple-element.103), channel_id=1, source_target_pairs={{0,1},{1,0},{2,3},{3,2},{4,5},{5,4},{6,7},{7,6},{8,9},{9,8},{10,11... | collective-permute-start | bytes 786440 | tf_op jit(solution)/shard_map/ppermute | solution.py:301
  33.7 3.0 %collective-permute-start.11 = (f32[256,128]{1,0:T(8,128)S(1)}, f32[256,128]{1,0:T(8,128)S(1)}, u32[]{:S(2)}, u32[]{:S(2)}) collective-permute-start(f32[256,128]{1,0:T(8,128)S(1)} %get-tuple-element.95), channel_id=1, source_target_pairs={{0,2},{2,0},{4,6},{6,4},{8,10},{10,8},{12,14},{14,12},{16,18},{18,... | collective-permute-start | bytes 393224 | tf_op jit(solution)/shard_map/ppermute | solution.py:301
  34.3 8.5 %collective-permute-start.16 = (f32[256,128]{1,0:T(8,128)S(1)}, f32[256,128]{1,0:T(8,128)S(1)}, u32[]{:S(2)}, u32[]{:S(2)}) collective-permute-start(f32[256,128]{1,0:T(8,128)S(1)} %get-tuple-element.107), channel_id=1, source_target_pairs={{0,4},{2,6},{4,0},{6,2},{8,12},{10,14},{12,8},{14,10},{16,20},{18,... | collective-permute-start | bytes 393224 | tf_op jit(solution)/shard_map/ppermute | solution.py:301
  36.4 7.7 %collective-permute-start.17 = (f32[256,128]{1,0:T(8,128)S(1)}, f32[256,128]{1,0:T(8,128)S(1)}, u32[]{:S(2)}, u32[]{:S(2)}) collective-permute-start(f32[256,128]{1,0:T(8,128)S(1)} %get-tuple-element.109), channel_id=1, source_target_pairs={{0,6},{2,4},{4,2},{6,0},{8,14},{10,12},{12,10},{14,8},{16,22},{18,... | collective-permute-start | bytes 393224 | tf_op jit(solution)/shard_map/ppermute | solution.py:301
  40.6 3.8 %collective-permute-start.15 = (f32[256,128]{1,0:T(8,128)S(1)}, f32[256,128]{1,0:T(8,128)S(1)}, u32[]{:S(2)}, u32[]{:S(2)}) collective-permute-start(f32[256,128]{1,0:T(8,128)S(1)} %get-tuple-element.106), channel_id=1, source_target_pairs={{0,2},{2,0},{4,6},{6,4},{8,10},{10,8},{12,14},{14,12},{16,18},{18,... | collective-permute-start | bytes 393224 | tf_op jit(solution)/shard_map/ppermute | solution.py:301
  40.7 6.4 %collective-permute-start.8 = (f32[256,128]{1,0:T(8,128)S(1)}, f32[256,128]{1,0:T(8,128)S(1)}, u32[]{:S(2)}, u32[]{:S(2)}) collective-permute-start(f32[256,128]{1,0:T(8,128)S(1)} %get-tuple-element.86), channel_id=1, source_target_pairs={{0,8},{2,10},{4,12},{6,14},{8,0},{10,2},{12,4},{14,6},{16,24},{18,... | collective-permute-start | bytes 393224 | tf_op jit(solution)/shard_map/ppermute | solution.py:301
  42.5 7.4 %collective-permute-start.19 = (f32[256,128]{1,0:T(8,128)S(1)}, f32[256,128]{1,0:T(8,128)S(1)}, u32[]{:S(2)}, u32[]{:S(2)}) collective-permute-start(f32[256,128]{1,0:T(8,128)S(1)} %get-tuple-element.99), channel_id=1, source_target_pairs={{0,8},{2,10},{4,12},{6,14},{8,0},{10,2},{12,4},{14,6},{16,24},{18,... | collective-permute-start | bytes 393224 | tf_op jit(solution)/shard_map/ppermute | solution.py:301
  42.8 9.9 %collective-permute-start.22 = (f32[256,128]{1,0:T(8,128)S(1)}, f32[256,128]{1,0:T(8,128)S(1)}, u32[]{:S(2)}, u32[]{:S(2)}) collective-permute-start(f32[256,128]{1,0:T(8,128)S(1)} %get-tuple-element.116), channel_id=1, source_target_pairs={{0,4},{2,6},{4,0},{6,2},{8,12},{10,14},{12,8},{14,10},{16,20},{18,... | collective-permute-start | bytes 393224 | tf_op jit(solution)/shard_map/ppermute | solution.py:301
  44.1 8.6 %collective-permute-start.23 = (f32[256,128]{1,0:T(8,128)S(1)}, f32[256,128]{1,0:T(8,128)S(1)}, u32[]{:S(2)}, u32[]{:S(2)}) collective-permute-start(f32[256,128]{1,0:T(8,128)S(1)} %get-tuple-element.118), channel_id=1, source_target_pairs={{0,6},{2,4},{4,2},{6,0},{8,14},{10,12},{12,10},{14,8},{16,22},{18,... | collective-permute-start | bytes 393224 | tf_op jit(solution)/shard_map/ppermute | solution.py:301
  44.4 10.9 %collective-permute-start.21 = (f32[256,128]{1,0:T(8,128)S(1)}, f32[256,128]{1,0:T(8,128)S(1)}, u32[]{:S(2)}, u32[]{:S(2)}) collective-permute-start(f32[256,128]{1,0:T(8,128)S(1)} %get-tuple-element.110), channel_id=1, source_target_pairs={{0,8},{2,10},{4,12},{6,14},{8,0},{10,2},{12,4},{14,6},{16,24},{18,... | collective-permute-start | bytes 393224 | tf_op jit(solution)/shard_map/ppermute | solution.py:301
  47.1 10.3 %collective-permute-start.18 = (f32[128,128]{1,0:T(8,128)S(1)}, f32[128,128]{1,0:T(8,128)S(1)}, u32[]{:S(2)}, u32[]{:S(2)}) collective-permute-start(f32[128,128]{1,0:T(8,128)S(1)} %slice_add_fusion.3), channel_id=1, source_target_pairs={{0,16},{2,18},{4,20},{6,22},{8,24},{10,26},{12,28},{14,30},{16,0},... | collective-permute-start | bytes 196616 | tf_op jit(solution)/shard_map/ppermute | solution.py:301
  49.9 7.4 %collective-permute-start.20 = (f32[128,128]{1,0:T(8,128)S(1)}, f32[128,128]{1,0:T(8,128)S(1)}, u32[]{:S(2)}, u32[]{:S(2)}) collective-permute-start(f32[128,128]{1,0:T(8,128)S(1)} %slice_add_fusion.2), channel_id=1, source_target_pairs={{0,16},{2,18},{4,20},{6,22},{8,24},{10,26},{12,28},{14,30},{16,0},... | collective-permute-start | bytes 196616 | tf_op jit(solution)/shard_map/ppermute | solution.py:301
  53.0 6.2 %collective-permute-start.25 = (f32[256,128]{1,0:T(8,128)S(1)}, f32[256,128]{1,0:T(8,128)S(1)}, u32[]{:S(2)}, u32[]{:S(2)}) collective-permute-start(f32[256,128]{1,0:T(8,128)S(1)} %get-tuple-element.119), channel_id=1, source_target_pairs={{0,8},{2,10},{4,12},{6,14},{8,0},{10,2},{12,4},{14,6},{16,24},{18,... | collective-permute-start | bytes 393224 | tf_op jit(solution)/shard_map/ppermute | solution.py:301
  55.3 6.3 %collective-permute-start.24 = (f32[128,128]{1,0:T(8,128)S(1)}, f32[128,128]{1,0:T(8,128)S(1)}, u32[]{:S(2)}, u32[]{:S(2)}) collective-permute-start(f32[128,128]{1,0:T(8,128)S(1)} %slice_add_fusion.1), channel_id=1, source_target_pairs={{0,16},{2,18},{4,20},{6,22},{8,24},{10,26},{12,28},{14,30},{16,0},... | collective-permute-start | bytes 196616 | tf_op jit(solution)/shard_map/ppermute | solution.py:301
  59.2 6.6 %collective-permute-start.26 = (f32[128,128]{1,0:T(8,128)S(1)}, f32[128,128]{1,0:T(8,128)S(1)}, u32[]{:S(2)}, u32[]{:S(2)}) collective-permute-start(f32[128,128]{1,0:T(8,128)S(1)} %slice_add_fusion), channel_id=1, source_target_pairs={{0,16},{2,18},{4,20},{6,22},{8,24},{10,26},{12,28},{14,30},{16,0},... | collective-permute-start | bytes 196616 | tf_op jit(solution)/shard_map/ppermute | solution.py:301
